TPU v7x, 32 devices: a whole 2x2x4 slice. The times are simulated.
32 devices in a mesh: corner: 8 (over z, x), space: 4 (over y, core).
Axes of the slice: x: 2, y: 2, z: 4, core: 2. Of those that a mesh axis runs over, the one named last changes fastest.
Arguments:
- design: float32 [192, 1024], P('space'), may hold values from 0 to 1
- corner_set: int32 [8], P('corner'), may hold values from 0 to 3
- corner_dose: float32 [8], P('corner'), may hold values from 0.7 to 1.4
- kernel_taps: float32 [4, 4, 8, 17], replicated, may hold values from -1 to 1, as said below
- kernel_weights: float32 [4, 8], replicated, may hold values from 0.1 to 1
- support_mask: int32 [192, 1024], P('space'), may hold values 0 or 1
- load_mask: int32 [192, 1024], P('space'), may hold values 0 or 1
- force: float32 [2], replicated, may hold values from 0.5 to 1.5
Outputs:
- sensitivity: float32 [192, 1024], P('space', 'corner')
Inputs may be any that keep to these rules, and one draw needn't show every extreme that they name: `kernel_taps`: entries 0 and 2 along the second dimension lie in 0.2 to 1.
All inputs are finite; a program needn't handle non-finite values. No bound on the sum of `support_mask` or of `load_mask` on one device may be relied on, other than what follows from the above.
Results may differ from a plain program's by a relative error of at most 0.0003.
Values sent between devices are 32-bit elements; how exact they have to be, the bound alone decides.
A program may use at most 128 MiB of HBM per device.

v0:
```python
import jax
import jax.numpy as jnp
from jax import lax
from jax.sharding import PartitionSpec as P

ITERS = 2


beta_sharp = 8.0
eta_level = 0.25
stiff_floor = 0.05
kappa_ground = 0.1
spring_support = 1.0
poisson_ratio = 0.3


def padded(cells, sides, width):
    for axis, dim in sides:
        count = lax.axis_size(axis)
        ends = count - 1
        head = lax.slice_in_dim(cells, 0, width, axis=dim)
        tail = lax.slice_in_dim(cells, cells.shape[dim] - width, cells.shape[dim], axis=dim)
        cells = jnp.concatenate(
            [
                lax.ppermute(tail, axis, [(i, (i + 1) % count) for i in range(ends)]),
                cells,
                lax.ppermute(head, axis, [((i + 1) % count, i) for i in range(ends)]),
            ],
            axis=dim,
        )
    return cells


def convolve(part_re, part_im, tap_re, tap_im, along, margin, flipped):
    extent = part_re.shape[along] - 2 * margin
    out_re = 0.0
    out_im = 0.0
    for offset in range(2 * margin + 1):
        begin_at = 2 * margin - offset if flipped else offset
        piece_re = lax.slice_in_dim(part_re, begin_at, begin_at + extent, axis=along)
        out_re = out_re + tap_re[offset] * piece_re
        out_im = out_im + tap_im[offset] * piece_re
        if part_im is not None:
            piece_im = lax.slice_in_dim(part_im, begin_at, begin_at + extent, axis=along)
            out_re = out_re - tap_im[offset] * piece_im
            out_im = out_im + tap_re[offset] * piece_im
    return (out_re, out_im)


def clear_field(tap_table, weights):
    tap_sums = jnp.sum(tap_table, axis=2)
    row_gain = tap_sums[0] * tap_sums[0] + tap_sums[1] * tap_sums[1]
    col_gain = tap_sums[2] * tap_sums[2] + tap_sums[3] * tap_sums[3]
    return jnp.sum(weights * row_gain * col_gain)


def spread_total():
    return jnp.tanh(beta_sharp * eta_level) + jnp.tanh(beta_sharp * (1.0 - eta_level))


def project(intensity):
    return (
        jnp.tanh(beta_sharp * eta_level) + jnp.tanh(beta_sharp * (intensity - eta_level))
    ) / spread_total()


def project_slope(intensity):
    inner_tanh = jnp.tanh(beta_sharp * (intensity - eta_level))
    return beta_sharp * (1.0 - inner_tanh * inner_tanh) / spread_total()


def harmonic(lower_side, upper_side):
    return 2.0 * lower_side * upper_side / (lower_side + upper_side)


def coefficients():
    shear = 0.5 * (1.0 - poisson_ratio)
    coef_row = jnp.array([1.0, shear]).reshape(2, 1, 1)
    coef_col = jnp.array([shear, 1.0]).reshape(2, 1, 1)
    return (coef_row, coef_col)


def operate(field_ext, stiff_ext, ground):
    coef_row, coef_col = coefficients()
    field_all = jnp.pad(field_ext, ((0, 0), (0, 0), (1, 1)))
    stiff_all = jnp.pad(stiff_ext, ((0, 0), (1, 1)))
    stiff_mid = stiff_all[:, 1:-1]
    face_row = harmonic(stiff_mid[:-1], stiff_mid[1:])
    flux_row = coef_row * face_row * (field_all[:, 1:, 1:-1] - field_all[:, :-1, 1:-1])
    stiff_inner = stiff_all[1:-1]
    face_col = harmonic(stiff_inner[:, :-1], stiff_inner[:, 1:])
    flux_col = coef_col * face_col * (field_all[:, 1:-1, 1:] - field_all[:, 1:-1, :-1])
    centre = field_all[:, 1:-1, 1:-1]
    return (
        ground * centre
        + flux_row[:, :-1]
        - flux_row[:, 1:]
        + flux_col[:, :, :-1]
        - flux_col[:, :, 1:]
    )


def stiffness_slope(field_ext, stiff_ext, field):
    coef_row, coef_col = coefficients()
    field_all = jnp.pad(field_ext, ((0, 0), (0, 0), (1, 1)))
    stiff_all = jnp.pad(stiff_ext, ((0, 0), (1, 1)))
    stiff_mid = stiff_all[:, 1:-1]
    lower_row = stiff_mid[:-1]
    upper_row = stiff_mid[1:]
    diff_row = field_all[:, 1:, 1:-1] - field_all[:, :-1, 1:-1]
    energy_row = jnp.sum(coef_row * diff_row * diff_row, axis=0)
    both_row = lower_row + upper_row
    to_lower = 2.0 * upper_row * upper_row / (both_row * both_row) * energy_row
    to_upper = 2.0 * lower_row * lower_row / (both_row * both_row) * energy_row
    row_part = to_upper[:-1] + to_lower[1:]
    stiff_inner = stiff_all[1:-1]
    lower_col = stiff_inner[:, :-1]
    upper_col = stiff_inner[:, 1:]
    diff_col = field_all[:, 1:-1, 1:] - field_all[:, 1:-1, :-1]
    energy_col = jnp.sum(coef_col * diff_col * diff_col, axis=0)
    both_col = lower_col + upper_col
    left_side = 2.0 * upper_col * upper_col / (both_col * both_col) * energy_col
    right_side = 2.0 * lower_col * lower_col / (both_col * both_col) * energy_col
    col_part = right_side[:, :-1] + left_side[:, 1:]
    return -(kappa_ground * jnp.sum(field * field, axis=0) + row_part + col_part)


def intensity_gain(slope, density, intensity, dose_level, clear_level):
    return (
        slope
        * (3.0 * (1.0 - stiff_floor))
        * density
        * density
        * project_slope(intensity)
        * dose_level
        / clear_level
    )


def displaced(field):
    return padded(field, (("space", 1),), 1)


def residual_norm(residual):
    return lax.psum(jnp.sum(residual * residual), "space")


def on_device(
    design, corner_set, corner_dose, kernel_taps, kernel_weights, support_mask, load_mask, force
):
    margin = kernel_taps.shape[3] // 2
    kernel_count = kernel_taps.shape[2]
    set_count = kernel_taps.shape[0]
    choose = (jnp.arange(set_count) == corner_set[0]).astype(jnp.float32)
    tap_table = jnp.sum(choose[:, None, None, None] * kernel_taps, axis=0)
    weights = jnp.sum(choose[:, None] * kernel_weights, axis=0)
    clear_level = clear_field(tap_table, weights)
    dose_level = corner_dose[0]
    design_ext = padded(design, (("space", 0),), margin)
    design_all = jnp.pad(design_ext, ((0, 0), (margin, margin)))
    fields = []
    intensity = jnp.zeros(design.shape, jnp.float32)
    for kernel in range(kernel_count):
        col_re, col_im = convolve(
            design_all, None, tap_table[2, kernel], tap_table[3, kernel], 1, margin, True
        )
        field_re, field_im = convolve(
            col_re, col_im, tap_table[0, kernel], tap_table[1, kernel], 0, margin, True
        )
        fields.append((field_re, field_im))
        intensity = intensity + weights[kernel] * (field_re * field_re + field_im * field_im)
    intensity = dose_level * intensity / clear_level
    density = project(intensity)
    stiff = stiff_floor + (1.0 - stiff_floor) * density * density * density
    stiff_ext = padded(stiff, (("space", 0),), 1)
    ground = kappa_ground * stiff + spring_support * support_mask.astype(jnp.float32)
    load_field = force[:, None, None] * load_mask.astype(jnp.float32)[None]
    solution = jnp.zeros_like(load_field)
    residual = load_field
    direction = load_field
    norm_now = residual_norm(residual)
    for step in range(ITERS):
        image = operate(displaced(direction), stiff_ext, ground)
        alpha = norm_now / lax.psum(jnp.sum(direction * image), "space")
        solution = solution + alpha * direction
        residual = residual - alpha * image
        if step + 1 < ITERS:
            norm_next = residual_norm(residual)
            direction = residual + norm_next / norm_now * direction
            norm_now = norm_next
    slope = stiffness_slope(displaced(solution), stiff_ext, solution)
    gain = intensity_gain(slope, density, intensity, dose_level, clear_level)
    term = jnp.zeros(design.shape, jnp.float32)
    for kernel in range(kernel_count):
        field_re, field_im = fields[kernel]
        back = padded(jnp.stack([field_re * gain, -field_im * gain]), (("space", 1),), margin)
        back_all = jnp.pad(back, ((0, 0), (0, 0), (margin, margin)))
        col_re, col_im = convolve(
            back_all[0], back_all[1], tap_table[2, kernel], tap_table[3, kernel], 1, margin, False
        )
        out_re, out_im = convolve(
            col_re, col_im, tap_table[0, kernel], tap_table[1, kernel], 0, margin, False
        )
        term = term + 2.0 * weights[kernel] * out_re
    return lax.psum_scatter(term, "corner", scatter_dimension=1, tiled=True)


def solution(mesh):
    placed = (
        P("space", None),
        P("corner"),
        P("corner"),
        P(),
        P(),
        P("space", None),
        P("space", None),
        P(),
    )
    return jax.shard_map(
        on_device, mesh=mesh, in_specs=placed, out_specs=P("space", "corner"), check_vma=False
    )
```

profile of v0, /device:TPU:0, one launch (start us, length us, event | category | flops | bytes accessed | tf_op | source)
XLA Modules:
  0.0 1222.5 jit_solution(12585826235614889765)
XLA Ops:
  12.8 4.5 collective-permute-start.5
  43.2 11.8 multiply_add_fusion.10
  55.0 11.4 multiply_add_fusion.11
  66.4 21.8 %multiply_add_fusion.25 = f32[48,1024]{1,0:T(8,128)S(1)} fusion(f32[64,1024]{1,0:T(8,128)S(1)} %multiply_add_fusion.10, f32[64,1024]{1,0:T(8,128)S(1)} %multiply_add_fusion.11, f32[]{:T(128)} %bitcast.484, f32[]{:T(128)} %bitcast.483, f32[]{:T(128)} %bitcast.482, f32[]{:T(128)} %bitcast.481, f32[]{:T(128)} %bitcast.480, f32[]{:T(128)} %bitcast.479, ...), kind=kLoop, calls=%fused_computation.747 | loop fusion | flops 3293184 | bytes 6881416 | tf_op jit(solution)/shard_map/add | solution.py:46
  88.1 21.8 %multiply_subtract_fusion.10 = f32[48,1024]{1,0:T(8,128)S(1)} fusion(f32[64,1024]{1,0:T(8,128)S(1)} %multiply_add_fusion.10, f32[64,1024]{1,0:T(8,128)S(1)} %multiply_add_fusion.11, f32[]{:T(128)} %bitcast.484, f32[]{:T(128)} %bitcast.483, f32[]{:T(128)} %bitcast.482, f32[]{:T(128)} %bitcast.481, f32[]{:T(128)} %bitcast.480, f32[]{:T(128)} %bitcast.479, ...), kind=kLoop, calls=%fused_computation.748 | loop fusion | flops 3293184 | bytes 6881416 | tf_op jit(solution)/shard_map/sub | solution.py:45
  109.9 11.7 multiply_add_fusion.9
  121.6 11.9 multiply_add_fusion.8
  133.4 21.7 %multiply_add_fusion.24 = f32[48,1024]{1,0:T(8,128)S(1)} fusion(f32[64,1024]{1,0:T(8,128)S(1)} %multiply_add_fusion.8, f32[64,1024]{1,0:T(8,128)S(1)} %multiply_add_fusion.9, f32[]{:T(128)} %bitcast.553, f32[]{:T(128)} %bitcast.552, f32[]{:T(128)} %bitcast.551, f32[]{:T(128)} %bitcast.550, f32[]{:T(128)} %bitcast.549, f32[]{:T(128)} %bitcast.548, ...), kind=kLoop, calls=%fused_computation.745 | loop fusion | flops 3293184 | bytes 6881416 | tf_op jit(solution)/shard_map/add | solution.py:46
  155.1 21.7 %multiply_subtract_fusion.9 = f32[48,1024]{1,0:T(8,128)S(1)} fusion(f32[64,1024]{1,0:T(8,128)S(1)} %multiply_add_fusion.8, f32[64,1024]{1,0:T(8,128)S(1)} %multiply_add_fusion.9, f32[]{:T(128)} %bitcast.553, f32[]{:T(128)} %bitcast.552, f32[]{:T(128)} %bitcast.551, f32[]{:T(128)} %bitcast.550, f32[]{:T(128)} %bitcast.549, f32[]{:T(128)} %bitcast.548, ...), kind=kLoop, calls=%fused_computation.746 | loop fusion | flops 3293184 | bytes 6881416 | tf_op jit(solution)/shard_map/sub | solution.py:45
  176.8 11.9 multiply_add_fusion.12
  188.8 11.5 multiply_add_fusion.13
  200.3 11.9 multiply_add_fusion.14
  212.2 11.6 multiply_add_fusion.15
  223.9 11.7 multiply_add_fusion.16
  235.6 11.9 multiply_add_fusion.17
  247.6 11.6 multiply_add_fusion.18
  259.2 11.8 multiply_add_fusion.19
  271.0 11.6 multiply_add_fusion.20
  282.7 11.7 multiply_add_fusion.21
  294.4 11.8 multiply_add_fusion.22
  306.2 11.9 multiply_add_fusion.23
  318.2 22.0 %multiply_add_fusion.26 = f32[48,1024]{1,0:T(8,128)S(1)} fusion(f32[64,1024]{1,0:T(8,128)S(1)} %multiply_add_fusion.12, f32[64,1024]{1,0:T(8,128)S(1)} %multiply_add_fusion.13, f32[]{:T(128)} %bitcast.415, f32[]{:T(128)} %bitcast.414, f32[]{:T(128)} %bitcast.413, f32[]{:T(128)} %bitcast.412, f32[]{:T(128)} %bitcast.411, f32[]{:T(128)} %bitcast.410, ...), kind=kLoop, calls=%fused_computation.749 | loop fusion | flops 3293184 | bytes 6881416 | tf_op jit(solution)/shard_map/add | solution.py:46
  341.1 150.0 %convert_add_fusion = (f32[48,1024]{1,0:T(8,128)S(1)}, f32[48,1024]{1,0:T(8,128)S(1)}, f32[48,1024]{1,0:T(8,128)}, f32[48,1024]{1,0:T(8,128)}, f32[48,1024]{1,0:...) fusion(s32[48,1024]{1,0:T(8,128)S(1)} %copy-done.16, ...), kind=kLoop, calls=%fused_computation.743 | loop fusion | flops 38780928 | bytes 43844440 | tf_op jit(solution)/shard_map/add | solution.py:176
  502.1 8.7 all-reduce.13
  512.9 6.3 psum.30
  528.4 8.7 psum.31
  550.5 4.8 collective-permute-start.12
  571.8 23.3 %multiply_add_fusion.6 = f32[64,1024]{1,0:T(8,128)S(1)} fusion(f32[64,1040]{1,0:T(8,128)S(1)} %get-tuple-element.30, f32[64,1040]{1,0:T(8,128)S(1)} %get-tuple-element.29, f32[]{:T(128)} %bitcast.107, f32[]{:T(128)} %bitcast.106, f32[]{:T(128)} %bitcast.105, f32[]{:T(128)} %bitcast.104, f32[]{:T(128)} %bitcast.103, f32[]{:T(128)} %bitcast.102, ...), kind=kLoop, calls=%fused_computation.126 | loop fusion | flops 4390912 | bytes 9175176 | tf_op jit(solution)/shard_map/add | solution.py:46
  595.1 23.3 %multiply_subtract_fusion.7 = f32[64,1024]{1,0:T(8,128)S(1)} fusion(f32[64,1040]{1,0:T(8,128)S(1)} %get-tuple-element.30, f32[64,1040]{1,0:T(8,128)S(1)} %get-tuple-element.29, f32[]{:T(128)} %bitcast.107, f32[]{:T(128)} %bitcast.106, f32[]{:T(128)} %bitcast.105, f32[]{:T(128)} %bitcast.104, f32[]{:T(128)} %bitcast.103, f32[]{:T(128)} %bitcast.102, ...), kind=kLoop, calls=%fused_computation.127 | loop fusion | flops 4390912 | bytes 9175176 | tf_op jit(solution)/shard_map/sub | solution.py:45
  623.2 23.7 %multiply_add_fusion.7 = f32[64,1024]{1,0:T(8,128)S(1)} fusion(f32[64,1040]{1,0:T(8,128)S(1)} %get-tuple-element.32, f32[64,1040]{1,0:T(8,128)S(1)} %get-tuple-element.31, f32[]{:T(128)} %bitcast.37, f32[]{:T(128)} %bitcast.36, f32[]{:T(128)} %bitcast.35, f32[]{:T(128)} %bitcast.34, f32[]{:T(128)} %bitcast.33, f32[]{:T(128)} %bitcast.32, f32[]{:T(128)} %bitcast.31, ...), kind=kLoop, calls=%fused_computation.128 | loop fusion | flops 4390912 | bytes 9175176 | tf_op jit(solution)/shard_map/add | solution.py:46
  646.9 23.7 %multiply_subtract_fusion.8 = f32[64,1024]{1,0:T(8,128)S(1)} fusion(f32[64,1040]{1,0:T(8,128)S(1)} %get-tuple-element.32, f32[64,1040]{1,0:T(8,128)S(1)} %get-tuple-element.31, f32[]{:T(128)} %bitcast.37, f32[]{:T(128)} %bitcast.36, f32[]{:T(128)} %bitcast.35, f32[]{:T(128)} %bitcast.34, f32[]{:T(128)} %bitcast.33, f32[]{:T(128)} %bitcast.32, f32[]{:T(128)} %bitcast.31, ...), kind=kLoop, calls=%fused_computation.129 | loop fusion | flops 4390912 | bytes 9175176 | tf_op jit(solution)/shard_map/sub | solution.py:45
  676.0 23.4 %multiply_add_fusion.5 = f32[64,1024]{1,0:T(8,128)S(1)} fusion(f32[64,1040]{1,0:T(8,128)S(1)} %get-tuple-element.34, f32[64,1040]{1,0:T(8,128)S(1)} %get-tuple-element.33, f32[]{:T(128)} %bitcast.176, f32[]{:T(128)} %bitcast.175, f32[]{:T(128)} %bitcast.174, f32[]{:T(128)} %bitcast.173, f32[]{:T(128)} %bitcast.172, f32[]{:T(128)} %bitcast.171, ...), kind=kLoop, calls=%fused_computation.124 | loop fusion | flops 4390912 | bytes 9175176 | tf_op jit(solution)/shard_map/add | solution.py:46
  699.4 23.4 %multiply_subtract_fusion.6 = f32[64,1024]{1,0:T(8,128)S(1)} fusion(f32[64,1040]{1,0:T(8,128)S(1)} %get-tuple-element.34, f32[64,1040]{1,0:T(8,128)S(1)} %get-tuple-element.33, f32[]{:T(128)} %bitcast.176, f32[]{:T(128)} %bitcast.175, f32[]{:T(128)} %bitcast.174, f32[]{:T(128)} %bitcast.173, f32[]{:T(128)} %bitcast.172, f32[]{:T(128)} %bitcast.171, ...), kind=kLoop, calls=%fused_computation.125 | loop fusion | flops 4390912 | bytes 9175176 | tf_op jit(solution)/shard_map/sub | solution.py:45
  722.9 4.3 collective-permute-start.18
  729.1 23.6 %multiply_add_fusion.4 = f32[64,1024]{1,0:T(8,128)S(1)} fusion(f32[64,1040]{1,0:T(8,128)S(1)} %get-tuple-element.36, f32[64,1040]{1,0:T(8,128)S(1)} %get-tuple-element.35, f32[]{:T(128)} %bitcast.245, f32[]{:T(128)} %bitcast.244, f32[]{:T(128)} %bitcast.243, f32[]{:T(128)} %bitcast.242, f32[]{:T(128)} %bitcast.241, f32[]{:T(128)} %bitcast.240, ...), kind=kLoop, calls=%fused_computation.122 | loop fusion | flops 4390912 | bytes 9175176 | tf_op jit(solution)/shard_map/add | solution.py:46
  752.7 23.6 %multiply_subtract_fusion.5 = f32[64,1024]{1,0:T(8,128)S(1)} fusion(f32[64,1040]{1,0:T(8,128)S(1)} %get-tuple-element.36, f32[64,1040]{1,0:T(8,128)S(1)} %get-tuple-element.35, f32[]{:T(128)} %bitcast.245, f32[]{:T(128)} %bitcast.244, f32[]{:T(128)} %bitcast.243, f32[]{:T(128)} %bitcast.242, f32[]{:T(128)} %bitcast.241, f32[]{:T(128)} %bitcast.240, ...), kind=kLoop, calls=%fused_computation.123 | loop fusion | flops 4390912 | bytes 9175176 | tf_op jit(solution)/shard_map/sub | solution.py:45
  782.2 23.2 %multiply_add_fusion.3 = f32[64,1024]{1,0:T(8,128)S(1)} fusion(f32[64,1040]{1,0:T(8,128)S(1)} %get-tuple-element.38, f32[64,1040]{1,0:T(8,128)S(1)} %get-tuple-element.37, f32[]{:T(128)} %bitcast.314, f32[]{:T(128)} %bitcast.313, f32[]{:T(128)} %bitcast.312, f32[]{:T(128)} %bitcast.311, f32[]{:T(128)} %bitcast.310, f32[]{:T(128)} %bitcast.309, ...), kind=kLoop, calls=%fused_computation.120 | loop fusion | flops 4390912 | bytes 9175176 | tf_op jit(solution)/shard_map/add | solution.py:46
  805.3 23.2 %multiply_subtract_fusion.4 = f32[64,1024]{1,0:T(8,128)S(1)} fusion(f32[64,1040]{1,0:T(8,128)S(1)} %get-tuple-element.38, f32[64,1040]{1,0:T(8,128)S(1)} %get-tuple-element.37, f32[]{:T(128)} %bitcast.314, f32[]{:T(128)} %bitcast.313, f32[]{:T(128)} %bitcast.312, f32[]{:T(128)} %bitcast.311, f32[]{:T(128)} %bitcast.310, f32[]{:T(128)} %bitcast.309, ...), kind=kLoop, calls=%fused_computation.121 | loop fusion | flops 4390912 | bytes 9175176 | tf_op jit(solution)/shard_map/sub | solution.py:45
  830.3 23.4 %multiply_add_fusion.2 = f32[64,1024]{1,0:T(8,128)S(1)} fusion(f32[64,1040]{1,0:T(8,128)S(1)} %get-tuple-element.40, f32[64,1040]{1,0:T(8,128)S(1)} %get-tuple-element.39, f32[]{:T(128)} %bitcast.383, f32[]{:T(128)} %bitcast.382, f32[]{:T(128)} %bitcast.381, f32[]{:T(128)} %bitcast.380, f32[]{:T(128)} %bitcast.379, f32[]{:T(128)} %bitcast.378, ...), kind=kLoop, calls=%fused_computation.118 | loop fusion | flops 4390912 | bytes 9175176 | tf_op jit(solution)/shard_map/add | solution.py:46
  853.7 23.4 %multiply_subtract_fusion.3 = f32[64,1024]{1,0:T(8,128)S(1)} fusion(f32[64,1040]{1,0:T(8,128)S(1)} %get-tuple-element.40, f32[64,1040]{1,0:T(8,128)S(1)} %get-tuple-element.39, f32[]{:T(128)} %bitcast.383, f32[]{:T(128)} %bitcast.382, f32[]{:T(128)} %bitcast.381, f32[]{:T(128)} %bitcast.380, f32[]{:T(128)} %bitcast.379, f32[]{:T(128)} %bitcast.378, ...), kind=kLoop, calls=%fused_computation.119 | loop fusion | flops 4390912 | bytes 9175176 | tf_op jit(solution)/shard_map/sub | solution.py:45
  877.3 23.1 %multiply_add_fusion.1 = f32[64,1024]{1,0:T(8,128)S(1)} fusion(f32[64,1040]{1,0:T(8,128)S(1)} %get-tuple-element.42, f32[64,1040]{1,0:T(8,128)S(1)} %get-tuple-element.41, f32[]{:T(128)} %bitcast.452, f32[]{:T(128)} %bitcast.451, f32[]{:T(128)} %bitcast.450, f32[]{:T(128)} %bitcast.449, f32[]{:T(128)} %bitcast.448, f32[]{:T(128)} %bitcast.447, ...), kind=kLoop, calls=%fused_computation.116 | loop fusion | flops 4390912 | bytes 9175176 | tf_op jit(solution)/shard_map/add | solution.py:46
  900.4 23.1 %multiply_subtract_fusion.2 = f32[64,1024]{1,0:T(8,128)S(1)} fusion(f32[64,1040]{1,0:T(8,128)S(1)} %get-tuple-element.42, f32[64,1040]{1,0:T(8,128)S(1)} %get-tuple-element.41, f32[]{:T(128)} %bitcast.452, f32[]{:T(128)} %bitcast.451, f32[]{:T(128)} %bitcast.450, f32[]{:T(128)} %bitcast.449, f32[]{:T(128)} %bitcast.448, f32[]{:T(128)} %bitcast.447, ...), kind=kLoop, calls=%fused_computation.117 | loop fusion | flops 4390912 | bytes 9175176 | tf_op jit(solution)/shard_map/sub | solution.py:45
  923.9 23.7 %multiply_add_fusion = f32[64,1024]{1,0:T(8,128)S(1)} fusion(f32[64,1040]{1,0:T(8,128)S(1)} %get-tuple-element.44, f32[64,1040]{1,0:T(8,128)S(1)} %get-tuple-element.43, f32[]{:T(128)} %bitcast.521, f32[]{:T(128)} %bitcast.520, f32[]{:T(128)} %bitcast.519, f32[]{:T(128)} %bitcast.518, f32[]{:T(128)} %bitcast.517, f32[]{:T(128)} %bitcast.516, f32[]{:T(128)} %bitcast.515, ...), kind=kLoop, calls=%fused_computation.114 | loop fusion | flops 4390912 | bytes 9175176 | tf_op jit(solution)/shard_map/add | solution.py:46
  947.6 23.5 %multiply_subtract_fusion.1 = f32[64,1024]{1,0:T(8,128)S(1)} fusion(f32[64,1040]{1,0:T(8,128)S(1)} %get-tuple-element.44, f32[64,1040]{1,0:T(8,128)S(1)} %get-tuple-element.43, f32[]{:T(128)} %bitcast.521, f32[]{:T(128)} %bitcast.520, f32[]{:T(128)} %bitcast.519, f32[]{:T(128)} %bitcast.518, f32[]{:T(128)} %bitcast.517, f32[]{:T(128)} %bitcast.516, ...), kind=kLoop, calls=%fused_computation.115 | loop fusion | flops 4390912 | bytes 9175176 | tf_op jit(solution)/shard_map/sub | solution.py:45
  971.0 4.4 fusion.274
  975.5 21.7 %fusion.281 = f32[48,1024]{1,0:T(8,128)S(1)} fusion(f32[64,1024]{1,0:T(8,128)S(1)} %multiply_add_fusion.7, f32[64,1024]{1,0:T(8,128)S(1)} %multiply_subtract_fusion.8, f32[]{:T(128)} %bitcast.69, f32[]{:T(128)} %bitcast.68, f32[]{:T(128)} %bitcast.67, f32[]{:T(128)} %bitcast.66, f32[]{:T(128)} %bitcast.65, f32[]{:T(128)} %bitcast.64, f32[]{:T(128)} %bitcast.63, ...), kind=kLoop, calls=%fused_computation.658 | loop fusion | flops 3342336 | bytes 6881420 | tf_op jit(solution)/shard_map/mul | solution.py:204
  997.2 155.4 %fusion.37 = f32[48,1024]{1,0:T(8,128)} fusion(f32[64,1024]{1,0:T(8,128)S(1)} %multiply_add_fusion, f32[64,1024]{1,0:T(8,128)S(1)} %multiply_subtract_fusion.1, f32[64,1024]{1,0:T(8,128)S(1)} %multiply_add_fusion.1, f32[64,1024]{1,0:T(8,128)S(1)} %multiply_subtract_fusion.2, f32[64,1024]{1,0:T(8,128)S(1)} %multiply_add_fusion.2, ...), kind=kLoop, calls=%fused_computation.176 | loop fusion | flops 23101440 | bytes 46007224 | tf_op jit(solution)/shard_map/add | solution.py:204
  1152.6 62.8 %reduce-scatter.2.cloned.1.call-done = f32[48,128]{1,0:T(8,128)} async-done(((f32[48,1024]{1,0:T(8,128)}), f32[48,128]{1,0:T(8,128)}) %reduce-scatter.2.cloned.1.call-update) | async-done | bytes 24592 | tf_op jit(solution)/shard_map/reduce_scatter | solution.py:205
  (184 shorter events, 94.8 us)
Async XLA Ops:
  6.5 1208.9 %reduce-scatter.2.cloned.1.call-start = ((), (), s32[]{:S(2)}) async-start(), calls=%async_computation.1 | async-start | bytes 221184 | tf_op jit(solution)/shard_map/reduce_scatter | solution.py:205
  7.3 35.8 %collective-permute-start.1 = (f32[8,1024]{1,0:T(8,128)S(1)}, f32[8,1024]{1,0:T(8,128)S(1)}, u32[]{:S(2)}, u32[]{:S(2)}) collective-permute-start(f32[8,1024]{1,0:T(8,128)S(1)} %get-tuple-element.92), channel_id=1, source_target_pairs={{1,0},{2,1},{3,2},{5,4},{6,5},{7,6},{9,8},{10,9},{11,10},{13,12},{... | collective-permute-start | bytes 98312 | tf_op jit(solution)/shard_map/ppermute | solution.py:27
  8.6 4.0 copy-start.18
  8.6 34.5 %collective-permute-start = (f32[8,1024]{1,0:T(8,128)S(1)}, f32[8,1024]{1,0:T(8,128)S(1)}, u32[]{:S(2)}, u32[]{:S(2)}) collective-permute-start(f32[8,1024]{1,0:T(8,128)S(1)} %get-tuple-element.93), channel_id=1, source_target_pairs={{0,1},{1,2},{2,3},{4,5},{5,6},{6,7},{8,9},{9,10},{10,11},{12,13},{... | collective-permute-start | bytes 98312 | tf_op jit(solution)/shard_map/ppermute | solution.py:25
  12.6 6.6 copy-start.17
  12.8 482.7 %collective-permute-start.5 = (f32[2,1,1024]{2,1,0:T(1,128)S(1)}, f32[2,1,1024]{2,1,0:T(1,128)S(1)}, u32[]{:S(2)}, u32[]{:S(2)}) collective-permute-start(f32[2,1,1024]{2,1,0:T(1,128)S(1)} %get-tuple-element.65), channel_id=1, source_target_pairs={{0,1},{1,2},{2,3},{4,5},{5,6},{6,7},{8,9},{9,10},{10,11},{12,13},{... | collective-permute-start | bytes 24584 | tf_op jit(solution)/shard_map/ppermute | solution.py:25
  17.3 478.2 %collective-permute-start.4 = (f32[2,1,1024]{2,1,0:T(1,128)S(1)}, f32[2,1,1024]{2,1,0:T(1,128)S(1)}, u32[]{:S(2)}, u32[]{:S(2)}) collective-permute-start(f32[2,1,1024]{2,1,0:T(1,128)S(1)} %get-tuple-element.66), channel_id=1, source_target_pairs={{1,0},{2,1},{3,2},{5,4},{6,5},{7,6},{9,8},{10,9},{11,10},{13,12},{... | collective-permute-start | bytes 24584 | tf_op jit(solution)/shard_map/ppermute | solution.py:27
  29.5 13.7 %copy-start.15 = (f32[48,1024]{1,0:T(8,128)S(1)}, f32[48,1024]{1,0:T(8,128)}, u32[]{:S(2)}) copy-start(f32[48,1024]{1,0:T(8,128)} %param.14) | copy-start | bytes 589828
  40.3 0.8 copy-start.21
  340.1 0.9 copy-start.16
  491.1 4.6 collective-permute-start.2
  494.2 4.3 collective-permute-start.3
  500.5 0.7 copy-start.20
  520.6 3.1 collective-permute-start.7
  522.4 4.6 collective-permute-start.6
  539.2 7.6 collective-permute-start.9
  540.6 6.3 collective-permute-start.8
  547.2 0.9 copy-start.2
  547.2 1.0 copy-start.14
  547.4 1.0 copy-start
  547.4 1.1 copy-start.1
  547.4 1.1 copy-start.13
  548.5 1.2 copy-start.3
  548.5 1.2 copy-start.4
  548.5 1.2 copy-start.5
  548.5 1.2 copy-start.6
  548.5 1.3 copy-start.7
  548.5 1.3 copy-start.8
  548.5 1.4 copy-start.9
  548.6 1.4 copy-start.10
  548.6 1.5 copy-start.11
  548.6 1.5 copy-start.12
  550.5 16.1 %collective-permute-start.12 = (f32[2,8,1024]{2,1,0:T(8,128)S(1)}, f32[2,8,1024]{2,1,0:T(8,128)S(1)}, u32[]{:S(2)}, u32[]{:S(2)}) collective-permute-start(f32[2,8,1024]{2,1,0:T(8,128)S(1)} %get-tuple-element.45), channel_id=1, source_target_pairs={{0,1},{1,2},{2,3},{4,5},{5,6},{6,7},{8,9},{9,10},{10,11},{12,13},{... | collective-permute-start | bytes 196616 | tf_op jit(solution)/shard_map/ppermute | solution.py:25
  555.3 15.0 %collective-permute-start.13 = (f32[2,8,1024]{2,1,0:T(8,128)S(1)}, f32[2,8,1024]{2,1,0:T(8,128)S(1)}, u32[]{:S(2)}, u32[]{:S(2)}) collective-permute-start(f32[2,8,1024]{2,1,0:T(8,128)S(1)} %get-tuple-element.46), channel_id=1, source_target_pairs={{1,0},{2,1},{3,2},{5,4},{6,5},{7,6},{9,8},{10,9},{11,10},{13,12},{... | collective-permute-start | bytes 196616 | tf_op jit(solution)/shard_map/ppermute | solution.py:27
  556.6 366.9 %collective-permute-start.24 = (f32[2,8,1024]{2,1,0:T(8,128)S(1)}, f32[2,8,1024]{2,1,0:T(8,128)S(1)}, u32[]{:S(2)}, u32[]{:S(2)}) collective-permute-start(f32[2,8,1024]{2,1,0:T(8,128)S(1)} %get-tuple-element.59), channel_id=1, source_target_pairs={{0,1},{1,2},{2,3},{4,5},{5,6},{6,7},{8,9},{9,10},{10,11},{12,13},{... | collective-permute-start | bytes 196616 | tf_op jit(solution)/shard_map/ppermute | solution.py:25
  560.9 362.7 %collective-permute-start.25 = (f32[2,8,1024]{2,1,0:T(8,128)S(1)}, f32[2,8,1024]{2,1,0:T(8,128)S(1)}, u32[]{:S(2)}, u32[]{:S(2)}) collective-permute-start(f32[2,8,1024]{2,1,0:T(8,128)S(1)} %get-tuple-element.60), channel_id=1, source_target_pairs={{1,0},{2,1},{3,2},{5,4},{6,5},{7,6},{9,8},{10,9},{11,10},{13,12},{... | collective-permute-start | bytes 196616 | tf_op jit(solution)/shard_map/ppermute | solution.py:27
  562.2 314.8 %collective-permute-start.22 = (f32[2,8,1024]{2,1,0:T(8,128)S(1)}, f32[2,8,1024]{2,1,0:T(8,128)S(1)}, u32[]{:S(2)}, u32[]{:S(2)}) collective-permute-start(f32[2,8,1024]{2,1,0:T(8,128)S(1)} %get-tuple-element.57), channel_id=1, source_target_pairs={{0,1},{1,2},{2,3},{4,5},{5,6},{6,7},{8,9},{9,10},{10,11},{12,13},{... | collective-permute-start | bytes 196616 | tf_op jit(solution)/shard_map/ppermute | solution.py:25
  566.6 51.8 %collective-permute-start.10 = (f32[2,8,1024]{2,1,0:T(8,128)S(1)}, f32[2,8,1024]{2,1,0:T(8,128)S(1)}, u32[]{:S(2)}, u32[]{:S(2)}) collective-permute-start(f32[2,8,1024]{2,1,0:T(8,128)S(1)} %get-tuple-element.47), channel_id=1, source_target_pairs={{0,1},{1,2},{2,3},{4,5},{5,6},{6,7},{8,9},{9,10},{10,11},{12,13},{... | collective-permute-start | bytes 196616 | tf_op jit(solution)/shard_map/ppermute | solution.py:25
  570.3 51.2 %collective-permute-start.11 = (f32[2,8,1024]{2,1,0:T(8,128)S(1)}, f32[2,8,1024]{2,1,0:T(8,128)S(1)}, u32[]{:S(2)}, u32[]{:S(2)}) collective-permute-start(f32[2,8,1024]{2,1,0:T(8,128)S(1)} %get-tuple-element.48), channel_id=1, source_target_pairs={{1,0},{2,1},{3,2},{5,4},{6,5},{7,6},{9,8},{10,9},{11,10},{13,12},{... | collective-permute-start | bytes 196616 | tf_op jit(solution)/shard_map/ppermute | solution.py:27
  618.4 52.2 %collective-permute-start.14 = (f32[2,8,1024]{2,1,0:T(8,128)S(1)}, f32[2,8,1024]{2,1,0:T(8,128)S(1)}, u32[]{:S(2)}, u32[]{:S(2)}) collective-permute-start(f32[2,8,1024]{2,1,0:T(8,128)S(1)} %get-tuple-element.49), channel_id=1, source_target_pairs={{0,1},{1,2},{2,3},{4,5},{5,6},{6,7},{8,9},{9,10},{10,11},{12,13},{... | collective-permute-start | bytes 196616 | tf_op jit(solution)/shard_map/ppermute | solution.py:25
  621.5 53.0 %collective-permute-start.15 = (f32[2,8,1024]{2,1,0:T(8,128)S(1)}, f32[2,8,1024]{2,1,0:T(8,128)S(1)}, u32[]{:S(2)}, u32[]{:S(2)}) collective-permute-start(f32[2,8,1024]{2,1,0:T(8,128)S(1)} %get-tuple-element.50), channel_id=1, source_target_pairs={{1,0},{2,1},{3,2},{5,4},{6,5},{7,6},{9,8},{10,9},{11,10},{13,12},{... | collective-permute-start | bytes 196616 | tf_op jit(solution)/shard_map/ppermute | solution.py:27
  670.7 52.2 %collective-permute-start.16 = (f32[2,8,1024]{2,1,0:T(8,128)S(1)}, f32[2,8,1024]{2,1,0:T(8,128)S(1)}, u32[]{:S(2)}, u32[]{:S(2)}) collective-permute-start(f32[2,8,1024]{2,1,0:T(8,128)S(1)} %get-tuple-element.51), channel_id=1, source_target_pairs={{0,1},{1,2},{2,3},{4,5},{5,6},{6,7},{8,9},{9,10},{10,11},{12,13},{... | collective-permute-start | bytes 196616 | tf_op jit(solution)/shard_map/ppermute | solution.py:25
  674.5 52.7 %collective-permute-start.17 = (f32[2,8,1024]{2,1,0:T(8,128)S(1)}, f32[2,8,1024]{2,1,0:T(8,128)S(1)}, u32[]{:S(2)}, u32[]{:S(2)}) collective-permute-start(f32[2,8,1024]{2,1,0:T(8,128)S(1)} %get-tuple-element.52), channel_id=1, source_target_pairs={{1,0},{2,1},{3,2},{5,4},{6,5},{7,6},{9,8},{10,9},{11,10},{13,12},{... | collective-permute-start | bytes 196616 | tf_op jit(solution)/shard_map/ppermute | solution.py:27
  722.9 53.5 %collective-permute-start.18 = (f32[2,8,1024]{2,1,0:T(8,128)S(1)}, f32[2,8,1024]{2,1,0:T(8,128)S(1)}, u32[]{:S(2)}, u32[]{:S(2)}) collective-permute-start(f32[2,8,1024]{2,1,0:T(8,128)S(1)} %get-tuple-element.53), channel_id=1, source_target_pairs={{0,1},{1,2},{2,3},{4,5},{5,6},{6,7},{8,9},{9,10},{10,11},{12,13},{... | collective-permute-start | bytes 196616 | tf_op jit(solution)/shard_map/ppermute | solution.py:25
  727.1 53.5 %collective-permute-start.19 = (f32[2,8,1024]{2,1,0:T(8,128)S(1)}, f32[2,8,1024]{2,1,0:T(8,128)S(1)}, u32[]{:S(2)}, u32[]{:S(2)}) collective-permute-start(f32[2,8,1024]{2,1,0:T(8,128)S(1)} %get-tuple-element.54), channel_id=1, source_target_pairs={{1,0},{2,1},{3,2},{5,4},{6,5},{7,6},{9,8},{10,9},{11,10},{13,12},{... | collective-permute-start | bytes 196616 | tf_op jit(solution)/shard_map/ppermute | solution.py:27
  776.3 52.2 %collective-permute-start.20 = (f32[2,8,1024]{2,1,0:T(8,128)S(1)}, f32[2,8,1024]{2,1,0:T(8,128)S(1)}, u32[]{:S(2)}, u32[]{:S(2)}) collective-permute-start(f32[2,8,1024]{2,1,0:T(8,128)S(1)} %get-tuple-element.55), channel_id=1, source_target_pairs={{0,1},{1,2},{2,3},{4,5},{5,6},{6,7},{8,9},{9,10},{10,11},{12,13},{... | collective-permute-start | bytes 196616 | tf_op jit(solution)/shard_map/ppermute | solution.py:25
  780.6 49.4 %collective-permute-start.21 = (f32[2,8,1024]{2,1,0:T(8,128)S(1)}, f32[2,8,1024]{2,1,0:T(8,128)S(1)}, u32[]{:S(2)}, u32[]{:S(2)}) collective-permute-start(f32[2,8,1024]{2,1,0:T(8,128)S(1)} %get-tuple-element.56), channel_id=1, source_target_pairs={{1,0},{2,1},{3,2},{5,4},{6,5},{7,6},{9,8},{10,9},{11,10},{13,12},{... | collective-permute-start | bytes 196616 | tf_op jit(solution)/shard_map/ppermute | solution.py:27
  828.5 48.5 %collective-permute-start.23 = (f32[2,8,1024]{2,1,0:T(8,128)S(1)}, f32[2,8,1024]{2,1,0:T(8,128)S(1)}, u32[]{:S(2)}, u32[]{:S(2)}) collective-permute-start(f32[2,8,1024]{2,1,0:T(8,128)S(1)} %get-tuple-element.58), channel_id=1, source_target_pairs={{1,0},{2,1},{3,2},{5,4},{6,5},{7,6},{9,8},{10,9},{11,10},{13,12},{... | collective-permute-start | bytes 196616 | tf_op jit(solution)/shard_map/ppermute | solution.py:27
  (1 other events, 0.7 us)
Sparse Core Ops, SparseCore 0:
  1152.7 62.6 reduce-scatter.1
where the time goes:
time: 1250 us; the launch traced here: 1220 us
  other arithmetic  1010 us (81%)
  waiting for transfers between devices  68.9 us (6%)
  starting transfers between devices  63.6 us (5%)
  local copies, waits for them, and re-layouts  27.1 us (2%)
  between operations  24.9 us (2%)
  blocking collectives  23.7 us (2%)
    add x11, other arithmetic, convolve(): out_im = out_im + tap_re[offset] * piece_im  253 us
    sub x10, other arithmetic, convolve(): out_re = out_re - tap_im[offset] * piece_im  231 us
    add x1, other arithmetic, on_device(): term = term + 2.0 * weights[kernel] * out_re  155 us
    add x1, other arithmetic, on_device(): kappa_ground * stiff + spring_support * support_mask.astype(jnp.float32)  150 us
    add x9, other arithmetic, convolve(): out_re = out_re + tap_re[offset] * piece_re  98 us
    add x8, other arithmetic, convolve(): out_im = out_im + tap_im[offset] * piece_re  94.3 us
    reduce_scatter x1, waiting for transfers between devices, on_device(): return lax.psum_scatter(term, 'corner', scatter_dimension=1, tiled=True)  62.8 us
    ppermute x13, starting transfers between devices, padded(): lax.ppermute(tail, axis, [(i, (i + 1) % count) for i in range(ends)])  46.1 us
  transfers between devices with their start and end apart: 27, of which 3 were waited for; matrix products, arithmetic and copies ran while one was open for 65% of the time, Pallas kernels for 0%

commit v1 on v0

v1 whole, which is shorter than its diff:
```python
import functools

import jax
import jax.numpy as jnp
from jax import lax
from jax.experimental import pallas as pl
from jax.experimental.pallas import tpu as pltpu
from jax.sharding import PartitionSpec as P

MESH = pl.DeviceIdType.MESH
LANES = 128
HALO = 24
MASK_HALO = 16
EDGE = 12
PAD = 8

beta_sharp = 8.0
eta_level = 0.25
stiff_floor = 0.05
kappa_ground = 0.1
shear = 0.35
bf16 = jnp.bfloat16
f32 = jnp.float32


def halves(value):
    high = value.astype(bf16)
    return high, (value - high.astype(f32)).astype(bf16)


def dot(left, right):
    return jnp.dot(left, right, preferred_element_type=f32)


def circulant(row, count, shift):
    turned = pltpu.roll(jnp.broadcast_to(row, (8, LANES)), shift, 1) if shift else row
    return pltpu.roll(
        jnp.broadcast_to(turned[:1], (count, LANES)), 0, 1, stride=1, stride_axis=0
    )


def side_lanes(blocks, at):
    zero = jnp.zeros_like(blocks[0])
    before = blocks[at - 1] if at > 0 else zero
    after = blocks[at + 1] if at + 1 < len(blocks) else zero
    lane = lax.broadcasted_iota(jnp.int32, zero.shape, 1)
    return jnp.where(lane < LANES // 2, after, before)


def kernel(
    n_space, n_corner, kernels, radius,
    set_ref, dose_ref, weight_ref, force_ref, design_ref, taps_ref, support_ref, load_ref,
    out_ref,
    tap_rows, base_plain, base_flip,
    col_hi, col_lo, back_col, row_hi, row_lo, back_row_hi, back_row_lo,
    halo, mask_halo, left_hi, left_lo, mid_hi, mid_lo, fields,
    stiff, ground, face_dn, face_rt, loads, image0, image1, factor, gain,
    total, term, share, shares, landed,
    halo_send, halo_recv, share_send, share_recv, term_send, term_recv,
):
    rows, columns = design_ref.shape
    span = rows + 2 * EDGE
    blocks = columns // LANES
    strips = span // 8
    me_s = lax.axis_index("space")
    me_c = lax.axis_index("corner")

    barrier = pltpu.get_barrier_semaphore()
    for off in range(1, n_space):
        pl.semaphore_signal(
            barrier, inc=1, device_id={"space": lax.rem(me_s + off, n_space)}, device_id_type=MESH
        )
    for off in range(1, n_corner):
        pl.semaphore_signal(
            barrier, inc=1, device_id={"corner": lax.rem(me_c + off, n_corner)}, device_id_type=MESH
        )

    chosen = set_ref[0]
    tap_rows[...] = jnp.zeros_like(tap_rows)
    for part in range(4):
        tap_rows[pl.ds(part * kernels, kernels), pl.ds(0, 2 * radius + 1)] = taps_ref[chosen, part]
    table = tap_rows[...]
    base_plain[...] = pltpu.roll(table, LANES - radius, 1)
    from_lane = lax.broadcasted_iota(jnp.int32, (LANES, LANES), 0)
    to_lane = lax.broadcasted_iota(jnp.int32, (LANES, LANES), 1)
    mirror = ((from_lane + to_lane) % LANES == radius).astype(f32)
    base_flip[...] = jnp.dot(
        table, mirror, preferred_element_type=f32, precision=lax.Precision.HIGHEST
    )
    sums = jnp.sum(table, axis=1, keepdims=True)
    sums = [sums[part * kernels:(part + 1) * kernels] for part in range(4)]
    which = lax.broadcasted_iota(jnp.int32, (kernels, 1), 0)
    weight_col = jnp.zeros((kernels, 1), f32)
    for at in range(kernels):
        weight_col = jnp.where(which == at, weight_ref[chosen, at], weight_col)
    clear = jnp.sum(
        weight_col
        * (sums[0] * sums[0] + sums[1] * sums[1])
        * (sums[2] * sums[2] + sums[3] * sums[3]),
        axis=0, keepdims=True,
    )
    dose = dose_ref[0]

    pl.semaphore_wait(barrier, n_space + n_corner - 2)

    def edge_copies(toward):
        other = lax.rem(me_s + (n_space - 1 if toward == 0 else 1), n_space)
        sent = []
        for which_one, (source, target, width) in enumerate((
            (design_ref, halo, HALO),
            (load_ref, mask_halo.at[0], MASK_HALO),
            (support_ref, mask_halo.at[1], MASK_HALO),
        )):
            begin = 0 if toward == 0 else rows - width
            sent.append(pltpu.make_async_remote_copy(
                src_ref=source.at[pl.ds(begin, width)],
                dst_ref=target.at[pl.ds(toward * width, width)],
                send_sem=halo_send.at[toward, which_one],
                recv_sem=halo_recv.at[toward, which_one],
                device_id={"space": other},
                device_id_type=MESH,
            ))
        return sent

    has_before = me_s > 0
    has_after = me_s < n_space - 1

    @pl.when(has_before)
    def _():
        for copy in edge_copies(0):
            copy.start()

    @pl.when(has_after)
    def _():
        for copy in edge_copies(1):
            copy.start()

    near = jnp.abs(from_lane - to_lane) <= radius
    lane_row = lax.broadcasted_iota(jnp.int32, (span, LANES), 1)
    lane_out = lax.broadcasted_iota(jnp.int32, (rows, LANES), 1)
    reach = rows + 2 * HALO

    def build(at, carry):
        def plain(part):
            return base_plain[pl.ds(part * kernels + at, 1), :]

        def flip(part):
            return base_flip[pl.ds(part * kernels + at, 1), :]

        for part in range(2):
            band = circulant(plain(2 + part), LANES, 0)
            hi, lo = halves(band)
            zero = jnp.zeros_like(hi)
            there = pl.ds(part * LANES, LANES)
            col_hi[at, pl.ds(0, LANES), there] = jnp.where(near, hi, zero)
            col_hi[at, pl.ds(LANES, LANES), there] = jnp.where(near, zero, hi)
            col_lo[at, pl.ds(0, LANES), there] = jnp.where(near, lo, zero)
            col_lo[at, pl.ds(LANES, LANES), there] = jnp.where(near, zero, lo)
            band = circulant(flip(2 + part), LANES, 0)
            hi, lo = halves(band)
            for value, lanes in ((hi, 0), (lo, LANES)):
                back_col[at, pl.ds(2 * part * LANES, LANES), pl.ds(lanes, LANES)] = jnp.where(near, value, zero)
                back_col[at, pl.ds((2 * part + 1) * LANES, LANES), pl.ds(lanes, LANES)] = jnp.where(near, zero, value)

        def joined(first, second, lane, width):
            turned = pltpu.roll(second, width, 1)
            left = jnp.where(lane < width, first, turned)
            right = jnp.where(lane < 2 * width - LANES, turned, 0.0)
            return jnp.concatenate([left, right], axis=1)

        def forward_rows(part):
            band = circulant(flip(part), span, LANES - EDGE)
            band = jnp.where(lane_row < rows + HALO, band, pltpu.roll(band, reach, 1))
            return jnp.where(lane_row < reach, band, 0.0)

        row_re = forward_rows(0)
        row_im = forward_rows(1)
        matrix = jnp.concatenate(
            [joined(row_re, -row_im, lane_row, reach), joined(row_im, row_re, lane_row, reach)], axis=0
        )
        hi, lo = halves(matrix)
        row_hi[at] = hi
        row_lo[at] = lo
        scale = 2.0 * weight_ref[chosen, at]
        row_re = circulant(plain(0), rows, EDGE) * scale
        row_im = circulant(plain(1), rows, EDGE) * scale
        matrix = jnp.concatenate(
            [joined(row_re, -row_im, lane_out, span), joined(-row_im, -row_re, lane_out, span)], axis=0
        )
        hi, lo = halves(matrix)
        back_row_hi[at] = hi
        back_row_lo[at] = lo
        return carry

    lax.fori_loop(0, kernels, build, 0)

    def columns_of(cells, begin):
        parts = [cells[:, at * LANES:(at + 1) * LANES] for at in range(blocks)]
        for at in range(blocks):
            whole = jnp.concatenate([parts[at], side_lanes(parts, at)], axis=1)
            hi, lo = halves(whole)
            left_hi[pl.ds(at * rows, rows), :] = hi
            left_lo[pl.ds(at * rows, rows), :] = lo

        def one(at, carry):
            value = (
                dot(left_hi[...], col_hi[at])
                + dot(left_hi[...], col_lo[at])
                + dot(left_lo[...], col_hi[at])
            )
            hi, lo = halves(value)
            for block in range(blocks):
                for part in range(2):
                    here = (slice(block * rows, (block + 1) * rows), slice(part * LANES, (part + 1) * LANES))
                    there = (at, pl.ds(part * reach + begin, rows), pl.ds(block * LANES, LANES))
                    mid_hi[there] = hi[here]
                    mid_lo[there] = lo[here]
            return carry

        lax.fori_loop(0, kernels, one, 0)

    columns_of(design_ref[...], 0)

    @pl.when(has_after)
    def _():
        for copy in edge_copies(0):
            copy.wait_recv()

    @pl.when(jnp.logical_not(has_after))
    def _():
        halo[pl.ds(0, HALO), :] = jnp.zeros((HALO, columns), f32)
        mask_halo[:, pl.ds(0, MASK_HALO), :] = jnp.zeros((2, MASK_HALO, columns), jnp.int32)

    @pl.when(has_before)
    def _():
        for copy in edge_copies(1):
            copy.wait_recv()

    @pl.when(jnp.logical_not(has_before))
    def _():
        halo[pl.ds(HALO, HALO), :] = jnp.zeros((HALO, columns), f32)
        mask_halo[:, pl.ds(MASK_HALO, MASK_HALO), :] = jnp.zeros((2, MASK_HALO, columns), jnp.int32)

    columns_of(halo[...], rows)

    def rows_of(at, carry):
        fields[at] = (
            dot(row_hi[at][:, :2 * reach], mid_hi[at])
            + dot(row_hi[at][:, :2 * reach], mid_lo[at])
            + dot(row_lo[at][:, :2 * reach], mid_hi[at])
        )
        return carry

    lax.fori_loop(0, kernels, rows_of, 0)

    zero_pad = jnp.zeros((PAD, columns), f32)
    for array in (stiff, face_dn, loads, image0, image1):
        array[pl.ds(0, PAD), :] = zero_pad
        array[pl.ds(PAD + span, PAD), :] = zero_pad
    for which_one, own, target, base in ((0, load_ref, loads, PAD), (1, support_ref, ground, 0)):
        target[pl.ds(base, EDGE), :] = mask_halo[which_one, pl.ds(2 * MASK_HALO - EDGE, EDGE), :].astype(f32)
        target[pl.ds(base + EDGE, rows), :] = own[...].astype(f32)
        target[pl.ds(base + EDGE + rows, EDGE), :] = mask_halo[which_one, pl.ds(0, EDGE), :].astype(f32)

    row_in = lax.broadcasted_iota(jnp.int32, (8, columns), 0)
    lane_in = lax.broadcasted_iota(jnp.int32, (8, columns), 1)
    first_row = me_s * rows - EDGE
    grid_rows = n_space * rows
    spread = jnp.tanh(beta_sharp * eta_level) + jnp.tanh(beta_sharp * (1.0 - eta_level))
    low_end = jnp.tanh(beta_sharp * eta_level)
    weights = [weight_ref[chosen, at] for at in range(kernels)]
    gain_scale = dose * (3.0 * (1.0 - stiff_floor) * beta_sharp) / (clear * spread)

    def strip_of(strip):
        return pl.multiple_of(strip * 8, 8)

    def row_above(array, begin, here):
        before = array[pl.ds(begin + PAD - 8, 8), :]
        return jnp.where(row_in == 0, pltpu.roll(before, 1, 0), pltpu.roll(here, 1, 0))

    def row_below(array, begin, here):
        after = array[pl.ds(begin + PAD + 8, 8), :]
        return jnp.where(row_in == 7, pltpu.roll(after, 7, 0), pltpu.roll(here, 7, 0))

    def project(strip, carry):
        begin = strip_of(strip)
        bright = jnp.zeros((8, columns), f32)
        for at in range(kernels):
            re = fields[at, pl.ds(begin, 8), :]
            im = fields[at, pl.ds(span + begin, 8), :]
            bright = bright + weights[at] * (re * re + im * im)
        bright = dose * bright / clear
        bent = jnp.tanh(beta_sharp * (bright - eta_level))
        density = (low_end + bent) / spread
        square = density * density
        grid_row = row_in + (first_row + begin)
        inside = (grid_row >= 0) & (grid_row < grid_rows)
        hard = jnp.where(inside, stiff_floor + (1.0 - stiff_floor) * square * density, 0.0)
        stiff[pl.ds(begin + PAD, 8), :] = hard
        ground[pl.ds(begin, 8), :] = kappa_ground * hard + ground[pl.ds(begin, 8), :]
        factor[pl.ds(begin, 8), :] = jnp.where(
            inside, -gain_scale * square * (1.0 - bent * bent), 0.0
        )
        return carry

    lax.fori_loop(0, strips, project, 0)

    def faces(strip, carry):
        begin = strip_of(strip)
        here = stiff[pl.ds(begin + PAD, 8), :]
        below = row_below(stiff, begin, here)
        face_dn[pl.ds(begin + PAD, 8), :] = 2.0 * here * below / jnp.maximum(here + below, 1e-20)
        right = pltpu.roll(here, columns - 1, 1)
        face = 2.0 * here * right / jnp.maximum(here + right, 1e-20)
        face_rt[pl.ds(begin, 8), :] = jnp.where(lane_in < columns - 1, face, 0.0)
        return carry

    lax.fori_loop(0, strips, faces, 0)

    force0 = force_ref[0]
    force1 = force_ref[1]

    def around(strip):
        begin = strip_of(strip)
        right = face_rt[pl.ds(begin, 8), :]
        down = face_dn[pl.ds(begin + PAD, 8), :]
        return row_above(face_dn, begin, down), down, pltpu.roll(right, 1, 1), right

    def three(array, strip):
        begin = strip_of(strip)
        here = array[pl.ds(begin + PAD, 8), :]
        return row_above(array, begin, here), here, row_below(array, begin, here)

    def own_rows(strip):
        row = row_in + strip_of(strip)
        return (row >= EDGE) & (row < EDGE + rows)

    def flows(above, here, below, sides):
        face_up, face_down, face_left, face_right = sides
        along_rows = face_up * (here - above) + face_down * (here - below)
        along_columns = face_left * (here - pltpu.roll(here, 1, 1)) + face_right * (
            here - pltpu.roll(here, columns - 1, 1)
        )
        return along_rows, along_columns

    def first_image(strip, carry):
        norm, energy = carry
        begin = strip_of(strip)
        above, here, below = three(loads, strip)
        along_rows, along_columns = flows(above, here, below, around(strip))
        held = ground[pl.ds(begin, 8), :] * here
        one = force0 * (held + along_rows + shear * along_columns)
        two = force1 * (held + shear * along_rows + along_columns)
        image0[pl.ds(begin + PAD, 8), :] = one
        image1[pl.ds(begin + PAD, 8), :] = two
        own = jnp.where(own_rows(strip), here, 0.0)
        return norm + own * own, energy + own * (force0 * one + force1 * two)

    blank = jnp.zeros((8, columns), f32)
    norm, energy = lax.fori_loop(0, strips, first_image, (blank, blank))

    def whole_sum(cells):
        return jnp.sum(jnp.sum(cells, axis=0, keepdims=True), axis=1, keepdims=True)

    norm = whole_sum(norm) * (force0 * force0 + force1 * force1)
    energy = whole_sum(energy)
    ratio = jnp.where(norm > 0.0, energy / jnp.where(norm > 0.0, norm, 1.0), 0.0)

    def second_image(strip, carry):
        sums = list(carry)
        sides = around(strip)
        load3 = three(loads, strip)
        held = ground[pl.ds(strip_of(strip), 8), :]
        keep = own_rows(strip)
        for array, push, of_rows, of_columns in (
            (image0, force0, 1.0, shear), (image1, force1, shear, 1.0)
        ):
            image3 = three(array, strip)
            lean = ratio * push
            above, here, below = [image3[at] - lean * load3[at] for at in range(3)]
            along_rows, along_columns = flows(above, here, below, sides)
            applied = held * here + of_rows * along_rows + of_columns * along_columns
            applied = jnp.where(keep, applied, 0.0)
            sums[0] = sums[0] + jnp.where(keep, here * here, 0.0)
            sums[1] = sums[1] + here * applied
            sums[2] = sums[2] + push * load3[1] * applied
        return tuple(sums)

    first_strip = EDGE // 8
    last_strip = (EDGE + rows + 7) // 8
    rest = lax.fori_loop(first_strip, last_strip, second_image, (blank, blank, blank))
    values = [norm, ratio] + [whole_sum(cells) for cells in rest]
    lane8 = lax.broadcasted_iota(jnp.int32, (8, LANES), 1)
    packed = jnp.zeros((8, LANES), f32)
    for at, value in enumerate(values):
        packed = jnp.where(lane8 == at, value, packed)
    share[...] = packed

    def share_copy(off):
        return pltpu.make_async_remote_copy(
            src_ref=share,
            dst_ref=shares.at[off - 1],
            send_sem=share_send.at[off - 1],
            recv_sem=share_recv.at[off - 1],
            device_id={"space": lax.rem(me_s + off, n_space)},
            device_id_type=MESH,
        )

    for off in range(1, n_space):
        share_copy(off).start()
    for off in range(1, n_space):
        share_copy(off).wait_recv()
    tables = [packed] + [shares[off - 1] for off in range(1, n_space)]
    lists = [[each[0:1, at:at + 1] for at in range(5)] for each in tables]
    norm_now = sum(each[0] for each in lists)
    centre = sum(each[0] * each[1] for each in lists) / norm_now
    spare = 0.0
    bend = 0.0
    for part_norm, part_ratio, part_spare, part_bend, part_cross in lists:
        shift = part_ratio - centre
        spare = spare + part_spare + shift * shift * part_norm
        bend = bend + part_bend + shift * (part_cross + part_spare) + shift * shift * part_ratio * part_norm
    inverse = 1.0 / centre
    norm_next = spare * inverse * inverse
    renew = norm_next / norm_now
    curve = bend * inverse * inverse - renew * norm_next * centre
    step = norm_next / curve
    of_load = inverse + step * (1.0 + renew)
    of_image = -step * inverse

    def slopes(strip, carry):
        begin = strip_of(strip)
        sides = around(strip)
        squares = [side * side for side in sides]
        load3 = three(loads, strip)
        here_stiff = stiff[pl.ds(begin + PAD, 8), :]
        held = jnp.zeros((8, columns), f32)
        bent = jnp.zeros((8, columns), f32)
        for array, push, of_rows, of_columns in (
            (image0, force0, 1.0, shear), (image1, force1, shear, 1.0)
        ):
            image3 = three(array, strip)
            above, here, below = [
                (of_load * push) * load3[at] + of_image * image3[at] for at in range(3)
            ]
            up = here - above
            down = here - below
            left = here - pltpu.roll(here, 1, 1)
            right = here - pltpu.roll(here, columns - 1, 1)
            held = held + here * here
            bent = (
                bent
                + of_rows * (squares[0] * (up * up) + squares[1] * (down * down))
                + of_columns * (squares[2] * (left * left) + squares[3] * (right * right))
            )
        bent = bent * 0.5 / jnp.maximum(here_stiff * here_stiff, 1e-6)
        gain[pl.ds(begin, 8), :] = factor[pl.ds(begin, 8), :] * (kappa_ground * held + bent)
        return carry

    lax.fori_loop(0, strips, slopes, 0)

    total[...] = jnp.zeros_like(total)

    def back(at, carry):
        scale = gain[...]
        sent = jnp.concatenate(
            [fields[at, pl.ds(0, span), :] * scale, -(fields[at, pl.ds(span, span), :] * scale)], axis=0
        )
        hi, lo = halves(sent)
        turned = (
            dot(back_row_hi[at][:, :2 * span], hi)
            + dot(back_row_hi[at][:, :2 * span], lo)
            + dot(back_row_lo[at][:, :2 * span], hi)
        )
        grids = []
        for part in range(2):
            piece = turned[part * rows:(part + 1) * rows]
            parts = [piece[:, block * LANES:(block + 1) * LANES] for block in range(blocks)]
            grids.append([
                jnp.concatenate([parts[block], side_lanes(parts, block)], axis=1)
                for block in range(blocks)
            ])
        whole = jnp.concatenate(
            [jnp.concatenate([grids[0][block], grids[1][block]], axis=1) for block in range(blocks)], axis=0
        )
        hi, lo = halves(whole)
        wide = dot(hi, back_col[at])
        total[...] += wide[:, :LANES] + wide[:, LANES:] + dot(lo, back_col[at][:, :LANES])
        return carry

    lax.fori_loop(0, kernels, back, 0)
    for block in range(blocks):
        term[block] = total[pl.ds(block * rows, rows), :]

    width = columns // n_corner
    per_block = LANES // width

    def term_copy(off):
        other = lax.rem(me_c + off, n_corner)
        return pltpu.make_async_remote_copy(
            src_ref=term.at[other // per_block],
            dst_ref=landed.at[off - 1],
            send_sem=term_send.at[off - 1],
            recv_sem=term_recv.at[off - 1],
            device_id={"corner": other},
            device_id_type=MESH,
        )

    for off in range(1, n_corner):
        term_copy(off).start()
    summed = term[me_c // per_block]
    for off in range(1, n_corner):
        term_copy(off).wait_recv()
        summed = summed + landed[off - 1]
    if per_block == 1:
        out_ref[...] = summed
    else:
        place = lax.rem(me_c, per_block)
        kept = jnp.zeros(out_ref.shape, f32)
        for at in range(per_block):
            kept = kept + jnp.where(place == at, 1.0, 0.0) * summed[:, at * width:(at + 1) * width]
        out_ref[...] = kept

    for off in range(1, n_corner):
        term_copy(off).wait_send()
    for off in range(1, n_space):
        share_copy(off).wait_send()

    @pl.when(has_before)
    def _():
        for copy in edge_copies(0):
            copy.wait_send()

    @pl.when(has_after)
    def _():
        for copy in edge_copies(1):
            copy.wait_send()


def on_device(
    n_space, n_corner,
    design, corner_set, corner_dose, kernel_taps, kernel_weights, support_mask, load_mask, force,
):
    rows, columns = design.shape
    kernels = kernel_taps.shape[2]
    radius = kernel_taps.shape[3] // 2
    span = rows + 2 * EDGE
    reach = rows + 2 * HALO
    blocks = columns // LANES
    padded_rows = span + 2 * PAD
    in_smem = pl.BlockSpec(memory_space=pltpu.SMEM)
    in_vmem = pl.BlockSpec(memory_space=pltpu.VMEM)
    scratch = [
        pltpu.VMEM((4 * kernels, LANES), f32),
        pltpu.VMEM((4 * kernels, LANES), f32),
        pltpu.VMEM((4 * kernels, LANES), f32),
        pltpu.VMEM((kernels, 2 * LANES, 2 * LANES), bf16),
        pltpu.VMEM((kernels, 2 * LANES, 2 * LANES), bf16),
        pltpu.VMEM((kernels, 4 * LANES, 2 * LANES), bf16),
        pltpu.VMEM((kernels, 2 * span, 2 * LANES), bf16),
        pltpu.VMEM((kernels, 2 * span, 2 * LANES), bf16),
        pltpu.VMEM((kernels, 2 * rows, 2 * LANES), bf16),
        pltpu.VMEM((kernels, 2 * rows, 2 * LANES), bf16),
        pltpu.VMEM((2 * HALO, columns), f32),
        pltpu.VMEM((2, 2 * MASK_HALO, columns), jnp.int32),
        pltpu.VMEM((blocks * rows, 2 * LANES), bf16),
        pltpu.VMEM((blocks * rows, 2 * LANES), bf16),
        pltpu.VMEM((kernels, 2 * reach, columns), bf16),
        pltpu.VMEM((kernels, 2 * reach, columns), bf16),
        pltpu.VMEM((kernels, 2 * span, columns), f32),
        pltpu.VMEM((padded_rows, columns), f32),
        pltpu.VMEM((span, columns), f32),
        pltpu.VMEM((padded_rows, columns), f32),
        pltpu.VMEM((span, columns), f32),
        pltpu.VMEM((padded_rows, columns), f32),
        pltpu.VMEM((padded_rows, columns), f32),
        pltpu.VMEM((padded_rows, columns), f32),
        pltpu.VMEM((span, columns), f32),
        pltpu.VMEM((span, columns), f32),
        pltpu.VMEM((blocks * rows, LANES), f32),
        pltpu.VMEM((blocks, rows, LANES), f32),
        pltpu.VMEM((8, LANES), f32),
        pltpu.VMEM((n_space - 1, 8, LANES), f32),
        pltpu.VMEM((n_corner - 1, rows, LANES), f32),
        pltpu.SemaphoreType.DMA((2, 3)),
        pltpu.SemaphoreType.DMA((2, 3)),
        pltpu.SemaphoreType.DMA((n_space - 1,)),
        pltpu.SemaphoreType.DMA((n_space - 1,)),
        pltpu.SemaphoreType.DMA((n_corner - 1,)),
        pltpu.SemaphoreType.DMA((n_corner - 1,)),
    ]
    return pl.pallas_call(
        functools.partial(kernel, n_space, n_corner, kernels, radius),
        out_shape=jax.ShapeDtypeStruct((rows, columns // n_corner), f32),
        in_specs=[in_smem] * 4 + [in_vmem] * 4,
        out_specs=in_vmem,
        scratch_shapes=scratch,
        compiler_params=pltpu.CompilerParams(
            collective_id=0, has_side_effects=True, vmem_limit_bytes=48 * 1024 * 1024
        ),
    )(
        corner_set, corner_dose, kernel_weights, force,
        design, kernel_taps, support_mask, load_mask,
    )


def solution(mesh):
    placed = (
        P("space", None),
        P("corner"),
        P("corner"),
        P(),
        P(),
        P("space", None),
        P("space", None),
        P(),
    )
    body = functools.partial(on_device, mesh.shape["space"], mesh.shape["corner"])
    return jax.shard_map(
        body, mesh=mesh, in_specs=placed, out_specs=P("space", "corner"), check_vma=False
    )
```

time: 1250 us -> 42.9 us (0.03); the launches traced: 1220 us -> 42.7 us
  other arithmetic: 1010 us -> 0 us
  waiting for transfers between devices: 68.9 us -> 0 us
  starting transfers between devices: 63.6 us -> 0 us
  Pallas kernels: 0 us -> 37.1 us
  blocking collectives: 23.7 us -> 0 us
  between operations: 24.9 us -> 1.37 us
  local copies, waits for them, and re-layouts: 27.1 us -> 4.23 us
    add x32 -> x0, other arithmetic: 751 us -> none  [the longest x11 253 us: convolve(): out_im = out_im + tap_re[offset] * piece_im]
    sub x10 -> x0, other arithmetic: 231 us -> none  [convolve(): out_re = out_re - tap_im[offset] * piece_im]
    ppermute x26 -> x0, starting transfers between devices: 63.6 us -> none  [the longest x13 46.1 us: padded(): lax.ppermute(tail, axis, [(i, (i + 1) % count) for i in range(ends)])]
    reduce_scatter x1 -> x0, waiting for transfers between devices: 62.8 us -> none  [on_device(): return lax.psum_scatter(term, 'corner', scatter_dimension=1, tiled=True)]
    pallas_call x0 -> x1, Pallas kernels: none -> 37.1 us  [on_device(): pl.pallas_call(functools.partial(kernel, n_space, n_corner, kernels, radi...]
    psum x3 -> x0, blocking collectives: 23.7 us -> none  [the longest x2 15 us: residual_norm(): return lax.psum(jnp.sum(residual * residual), 'space')]
    mul x8 -> x0, other arithmetic: 23.4 us -> none  [the longest x1 21.7 us: on_device(): term = term + 2.0 * weights[kernel] * out_re]
    slice x36 -> x0, local copies, waits for them, and re-layouts: 23.1 us -> none  [the longest x20 14.4 us: convolve(): out_re = out_re + tap_re[offset] * piece_re]
  transfers between devices with their start and end apart: 27 -> 0, of which waited for: 3 -> 0; matrix products, arithmetic and copies ran while one was open for 65% -> 0% of each run, Pallas kernels for 0% -> 0%
where the time goes in v1:
time: 42.9 us; the launch traced here: 42.7 us
  Pallas kernels  37.1 us (86%)
  local copies, waits for them, and re-layouts  4.23 us (10%)
  between operations  1.37 us (3%)
    pallas_call x1, Pallas kernels, on_device(): pl.pallas_call(functools.partial(kernel, n_space, n_corner, kernels, radi...  37.1 us
    unnamed x13, local copies, waits for them, and re-layouts  4.23 us

profile of v1, /device:TPU:0, one launch (start us, length us, event | category | flops | bytes accessed | tf_op | source)
XLA Modules:
  0.0 42.7 jit_solution(7954945251516902359)
XLA Ops:
  0.0 0.0 copy-start.4
  0.7 0.0 copy-start.5
  1.3 0.0 copy-done.4
  1.3 0.0 copy-done.5
  1.4 0.0 copy-start
  1.4 0.9 %copy-done = f32[48,1024]{1,0:T(8,128)S(1)} copy-done((f32[48,1024]{1,0:T(8,128)S(1)}, f32[48,1024]{1,0:T(8,128)}, u32[]{:S(2)}) %copy-start) | copy-done | bytes 196632
  2.3 0.0 copy-start.1
  2.3 0.9 %copy-done.1 = s32[48,1024]{1,0:T(8,128)S(1)} copy-done((s32[48,1024]{1,0:T(8,128)S(1)}, s32[48,1024]{1,0:T(8,128)}, u32[]{:S(2)}) %copy-start.1) | copy-done | bytes 196632
  3.2 0.0 copy-start.2
  3.2 0.9 %copy-done.2 = s32[48,1024]{1,0:T(8,128)S(1)} copy-done((s32[48,1024]{1,0:T(8,128)S(1)}, s32[48,1024]{1,0:T(8,128)}, u32[]{:S(2)}) %copy-start.2) | copy-done | bytes 196632
  4.1 0.0 copy-start.3
  4.1 0.8 %copy-done.3 = f32[4,4,8,17]{3,2,1,0:T(8,128)S(1)} copy-done((f32[4,4,8,17]{3,2,1,0:T(8,128)S(1)}, f32[4,4,8,17]{3,2,1,0:T(8,128)}, u32[]{:S(2)}) %copy-start.3) | copy-done | bytes 8728
  5.0 37.1 %shard_map.82 = f32[48,128]{1,0:T(8,128)S(1)} custom-call(s32[1]{0:T(128)S(6)} %copy.10.set_ref, f32[1]{0:T(128)S(6)} %copy.11.dose_ref, f32[4,8]{1,0:T(4,128)S(1)} %copy-done.4, f32[2]{0:T(128)S(1)} %copy-done.5, f32[48,1024]{1,0:T(8,128)S(1)} %copy-done, f32[4,4,8,17]{3,2,1,0:T(8,128)S(1)} %copy-done.3, s32[48,1024]{1,0:T(8,128)S(1)} %copy-done.1, ...), custom_call_target="tpu_custom_call" | custom-call | tf_op jit(solution)/shard_map/pallas_call | solution.py:592
  42.1 0.6 %copy.12 = f32[48,128]{1,0:T(8,128)} copy(f32[48,128]{1,0:T(8,128)S(1)} %shard_map.82) | data formatting | bytes 49152
Async XLA Ops:
  0.0 1.3 %copy-start.4 = (f32[4,8]{1,0:T(4,128)S(1)}, f32[4,8]{1,0:T(4,128)}, u32[]{:S(2)}) copy-start(f32[4,8]{1,0:T(4,128)} %weight_ref.1) | copy-start | bytes 388
  0.7 0.7 %copy-start.5 = (f32[2]{0:T(128)S(1)}, f32[2]{0:T(128)}, u32[]{:S(2)}) copy-start(f32[2]{0:T(128)} %force_ref.1) | copy-start | bytes 28
  1.4 0.9 %copy-start = (f32[48,1024]{1,0:T(8,128)S(1)}, f32[48,1024]{1,0:T(8,128)}, u32[]{:S(2)}) copy-start(f32[48,1024]{1,0:T(8,128)} %design_ref.1) | copy-start | bytes 589828
  2.3 0.9 %copy-start.1 = (s32[48,1024]{1,0:T(8,128)S(1)}, s32[48,1024]{1,0:T(8,128)}, u32[]{:S(2)}) copy-start(s32[48,1024]{1,0:T(8,128)} %support_ref.1) | copy-start | bytes 589828
  3.2 0.9 %copy-start.2 = (s32[48,1024]{1,0:T(8,128)S(1)}, s32[48,1024]{1,0:T(8,128)}, u32[]{:S(2)}) copy-start(s32[48,1024]{1,0:T(8,128)} %load_ref.1) | copy-start | bytes 589828
  4.1 0.8 %copy-start.3 = (f32[4,4,8,17]{3,2,1,0:T(8,128)S(1)}, f32[4,4,8,17]{3,2,1,0:T(8,128)}, u32[]{:S(2)}) copy-start(f32[4,4,8,17]{3,2,1,0:T(8,128)} %taps_ref.1) | copy-start | bytes 26116

commit v2 on v1

--- a/solution.py
+++ b/solution.py
@@ -1,4 +1,5 @@
 import functools
+import math
 
 import jax
 import jax.numpy as jnp
@@ -49,15 +50,25 @@
 
 def kernel(
     n_space, n_corner, kernels, radius,
+    set_any, dose_any, weight_any, force_any, design_any, taps_any, support_any, load_any,
+    out_ref,
     set_ref, dose_ref, weight_ref, force_ref, design_ref, taps_ref, support_ref, load_ref,
-    out_ref,
     tap_rows, base_plain, base_flip,
-    col_hi, col_lo, back_col, row_hi, row_lo, back_row_hi, back_row_lo,
-    halo, mask_halo, left_hi, left_lo, mid_hi, mid_lo, fields,
+    col_all, back_col, row_both, back_row_both,
+    halo, mask_halo, left_all, mid_hi, mid_lo, fields, back_hi, back_lo,
     stiff, ground, face_dn, face_rt, loads, image0, image1, factor, gain,
-    total, term, share, shares, landed,
-    halo_send, halo_recv, share_send, share_recv, term_send, term_recv,
+    term, share, shares, landed,
+    local_sem, halo_send, halo_recv, share_send, share_recv, term_send, term_recv,
 ):
+    local = [
+        pltpu.make_async_copy(source, target, local_sem.at[at])
+        for at, (source, target) in enumerate((
+            (taps_any, taps_ref), (set_any, set_ref), (dose_any, dose_ref), (weight_any, weight_ref),
+            (force_any, force_ref), (design_any, design_ref), (load_any, load_ref), (support_any, support_ref),
+        ))
+    ]
+    for copy in local:
+        copy.start()
     rows, columns = design_ref.shape
     span = rows + 2 * EDGE
     blocks = columns // LANES
@@ -74,6 +85,43 @@
         pl.semaphore_signal(
             barrier, inc=1, device_id={"corner": lax.rem(me_c + off, n_corner)}, device_id_type=MESH
         )
+
+    pl.semaphore_wait(barrier, n_space + n_corner - 2)
+
+    def edge_copies(toward):
+        other = lax.rem(me_s + (n_space - 1 if toward == 0 else 1), n_space)
+        sent = []
+        for which_one, (source, target, width) in enumerate((
+            (design_any, halo, HALO),
+            (load_any, mask_halo.at[0], MASK_HALO),
+            (support_any, mask_halo.at[1], MASK_HALO),
+        )):
+            begin = 0 if toward == 0 else rows - width
+            sent.append(pltpu.make_async_remote_copy(
+                src_ref=source.at[pl.ds(begin, width)],
+                dst_ref=target.at[pl.ds(toward * width, width)],
+                send_sem=halo_send.at[toward, which_one],
+                recv_sem=halo_recv.at[toward, which_one],
+                device_id={"space": other},
+                device_id_type=MESH,
+            ))
+        return sent
+
+    has_before = me_s > 0
+    has_after = me_s < n_space - 1
+
+    @pl.when(has_before)
+    def _():
+        for copy in edge_copies(0):
+            copy.start()
+
+    @pl.when(has_after)
+    def _():
+        for copy in edge_copies(1):
+            copy.start()
+
+    for copy in local[:5]:
+        copy.wait()
 
     chosen = set_ref[0]
     tap_rows[...] = jnp.zeros_like(tap_rows)
@@ -101,40 +149,6 @@
     )
     dose = dose_ref[0]
 
-    pl.semaphore_wait(barrier, n_space + n_corner - 2)
-
-    def edge_copies(toward):
-        other = lax.rem(me_s + (n_space - 1 if toward == 0 else 1), n_space)
-        sent = []
-        for which_one, (source, target, width) in enumerate((
-            (design_ref, halo, HALO),
-            (load_ref, mask_halo.at[0], MASK_HALO),
-            (support_ref, mask_halo.at[1], MASK_HALO),
-        )):
-            begin = 0 if toward == 0 else rows - width
-            sent.append(pltpu.make_async_remote_copy(
-                src_ref=source.at[pl.ds(begin, width)],
-                dst_ref=target.at[pl.ds(toward * width, width)],
-                send_sem=halo_send.at[toward, which_one],
-                recv_sem=halo_recv.at[toward, which_one],
-                device_id={"space": other},
-                device_id_type=MESH,
-            ))
-        return sent
-
-    has_before = me_s > 0
-    has_after = me_s < n_space - 1
-
-    @pl.when(has_before)
-    def _():
-        for copy in edge_copies(0):
-            copy.start()
-
-    @pl.when(has_after)
-    def _():
-        for copy in edge_copies(1):
-            copy.start()
-
     near = jnp.abs(from_lane - to_lane) <= radius
     lane_row = lax.broadcasted_iota(jnp.int32, (span, LANES), 1)
     lane_out = lax.broadcasted_iota(jnp.int32, (rows, LANES), 1)
@@ -152,15 +166,15 @@
             hi, lo = halves(band)
             zero = jnp.zeros_like(hi)
             there = pl.ds(part * LANES, LANES)
-            col_hi[at, pl.ds(0, LANES), there] = jnp.where(near, hi, zero)
-            col_hi[at, pl.ds(LANES, LANES), there] = jnp.where(near, zero, hi)
-            col_lo[at, pl.ds(0, LANES), there] = jnp.where(near, lo, zero)
-            col_lo[at, pl.ds(LANES, LANES), there] = jnp.where(near, zero, lo)
+            for place, value in ((0, hi), (1, lo), (2, hi)):
+                col_all[at, pl.ds(2 * place * LANES, LANES), there] = jnp.where(near, value, zero)
+                col_all[at, pl.ds((2 * place + 1) * LANES, LANES), there] = jnp.where(near, zero, value)
             band = circulant(flip(2 + part), LANES, 0)
             hi, lo = halves(band)
             for value, lanes in ((hi, 0), (lo, LANES)):
-                back_col[at, pl.ds(2 * part * LANES, LANES), pl.ds(lanes, LANES)] = jnp.where(near, value, zero)
-                back_col[at, pl.ds((2 * part + 1) * LANES, LANES), pl.ds(lanes, LANES)] = jnp.where(near, zero, value)
+                place = pl.multiple_of(at * (4 * LANES), LANES) + 2 * part * LANES
+                back_col[pl.ds(place, LANES), pl.ds(lanes, LANES)] = jnp.where(near, value, zero)
+                back_col[pl.ds(place + LANES, LANES), pl.ds(lanes, LANES)] = jnp.where(near, zero, value)
 
         def joined(first, second, lane, width):
             turned = pltpu.roll(second, width, 1)
@@ -179,8 +193,8 @@
             [joined(row_re, -row_im, lane_row, reach), joined(row_im, row_re, lane_row, reach)], axis=0
         )
         hi, lo = halves(matrix)
-        row_hi[at] = hi
-        row_lo[at] = lo
+        row_both[at, pl.ds(0, 2 * span), :] = hi
+        row_both[at, pl.ds(2 * span, 2 * span), :] = lo
         scale = 2.0 * weight_ref[chosen, at]
         row_re = circulant(plain(0), rows, EDGE) * scale
         row_im = circulant(plain(1), rows, EDGE) * scale
@@ -188,8 +202,8 @@
             [joined(row_re, -row_im, lane_out, span), joined(-row_im, -row_re, lane_out, span)], axis=0
         )
         hi, lo = halves(matrix)
-        back_row_hi[at] = hi
-        back_row_lo[at] = lo
+        back_row_both[at, pl.ds(0, 2 * rows), :] = hi
+        back_row_both[at, pl.ds(2 * rows, 2 * rows), :] = lo
         return carry
 
     lax.fori_loop(0, kernels, build, 0)
@@ -199,15 +213,10 @@
         for at in range(blocks):
             whole = jnp.concatenate([parts[at], side_lanes(parts, at)], axis=1)
             hi, lo = halves(whole)
-            left_hi[pl.ds(at * rows, rows), :] = hi
-            left_lo[pl.ds(at * rows, rows), :] = lo
-
-        def one(at, carry):
-            value = (
-                dot(left_hi[...], col_hi[at])
-                + dot(left_hi[...], col_lo[at])
-                + dot(left_lo[...], col_hi[at])
-            )
+            left_all[pl.ds(at * rows, rows), :] = jnp.concatenate([hi, hi, lo], axis=1)
+
+        for at in range(kernels):
+            value = dot(left_all[...], col_all[at])
             hi, lo = halves(value)
             for block in range(blocks):
                 for part in range(2):
@@ -215,10 +224,8 @@
                     there = (at, pl.ds(part * reach + begin, rows), pl.ds(block * LANES, LANES))
                     mid_hi[there] = hi[here]
                     mid_lo[there] = lo[here]
-            return carry
-
-        lax.fori_loop(0, kernels, one, 0)
-
+
+    local[5].wait()
     columns_of(design_ref[...], 0)
 
     @pl.when(has_after)
@@ -243,15 +250,13 @@
 
     columns_of(halo[...], rows)
 
-    def rows_of(at, carry):
-        fields[at] = (
-            dot(row_hi[at][:, :2 * reach], mid_hi[at])
-            + dot(row_hi[at][:, :2 * reach], mid_lo[at])
-            + dot(row_lo[at][:, :2 * reach], mid_hi[at])
-        )
-        return carry
-
-    lax.fori_loop(0, kernels, rows_of, 0)
+    for at in range(kernels):
+        both = row_both[at][:, :2 * reach]
+        of_high = dot(both, mid_hi[at])
+        fields[at] = of_high[:2 * span] + of_high[2 * span:] + dot(both[:2 * span], mid_lo[at])
+
+    for copy in local[6:]:
+        copy.wait()
 
     zero_pad = jnp.zeros((PAD, columns), f32)
     for array in (stiff, face_dn, loads, image0, image1):
@@ -266,10 +271,11 @@
     lane_in = lax.broadcasted_iota(jnp.int32, (8, columns), 1)
     first_row = me_s * rows - EDGE
     grid_rows = n_space * rows
-    spread = jnp.tanh(beta_sharp * eta_level) + jnp.tanh(beta_sharp * (1.0 - eta_level))
-    low_end = jnp.tanh(beta_sharp * eta_level)
+    low_end = math.tanh(beta_sharp * eta_level)
+    spread = low_end + math.tanh(beta_sharp * (1.0 - eta_level))
     weights = [weight_ref[chosen, at] for at in range(kernels)]
-    gain_scale = dose * (3.0 * (1.0 - stiff_floor) * beta_sharp) / (clear * spread)
+    level = dose / clear
+    gain_scale = level * (3.0 * (1.0 - stiff_floor) * beta_sharp / spread)
 
     def strip_of(strip):
         return pl.multiple_of(strip * 8, 8)
@@ -289,9 +295,9 @@
             re = fields[at, pl.ds(begin, 8), :]
             im = fields[at, pl.ds(span + begin, 8), :]
             bright = bright + weights[at] * (re * re + im * im)
-        bright = dose * bright / clear
+        bright = bright * level
         bent = jnp.tanh(beta_sharp * (bright - eta_level))
-        density = (low_end + bent) / spread
+        density = (low_end + bent) * (1.0 / spread)
         square = density * density
         grid_row = row_in + (first_row + begin)
         inside = (grid_row >= 0) & (grid_row < grid_rows)
@@ -459,58 +465,62 @@
 
     lax.fori_loop(0, strips, slopes, 0)
 
-    total[...] = jnp.zeros_like(total)
-
-    def back(at, carry):
+    for at in range(kernels):
         scale = gain[...]
         sent = jnp.concatenate(
             [fields[at, pl.ds(0, span), :] * scale, -(fields[at, pl.ds(span, span), :] * scale)], axis=0
         )
         hi, lo = halves(sent)
-        turned = (
-            dot(back_row_hi[at][:, :2 * span], hi)
-            + dot(back_row_hi[at][:, :2 * span], lo)
-            + dot(back_row_lo[at][:, :2 * span], hi)
-        )
-        grids = []
+        both = back_row_both[at][:, :2 * span]
+        of_high = dot(both, hi)
+        turned = of_high[:2 * rows] + of_high[2 * rows:] + dot(both[:2 * rows], lo)
         for part in range(2):
             piece = turned[part * rows:(part + 1) * rows]
             parts = [piece[:, block * LANES:(block + 1) * LANES] for block in range(blocks)]
-            grids.append([
-                jnp.concatenate([parts[block], side_lanes(parts, block)], axis=1)
-                for block in range(blocks)
-            ])
-        whole = jnp.concatenate(
-            [jnp.concatenate([grids[0][block], grids[1][block]], axis=1) for block in range(blocks)], axis=0
-        )
-        hi, lo = halves(whole)
-        wide = dot(hi, back_col[at])
-        total[...] += wide[:, :LANES] + wide[:, LANES:] + dot(lo, back_col[at][:, :LANES])
-        return carry
-
-    lax.fori_loop(0, kernels, back, 0)
-    for block in range(blocks):
-        term[block] = total[pl.ds(block * rows, rows), :]
+            for block in range(blocks):
+                hi, lo = halves(jnp.concatenate([parts[block], side_lanes(parts, block)], axis=1))
+                lanes = pl.ds((2 * at + part) * 2 * LANES, 2 * LANES)
+                back_hi[block, :, lanes] = hi
+                back_lo[block, :, lanes] = lo
 
     width = columns // n_corner
     per_block = LANES // width
-
-    def term_copy(off):
-        other = lax.rem(me_c + off, n_corner)
+    my_block = me_c // per_block
+
+    def term_copy(block, other, sent_as):
+        slot = lax.rem(other - me_c + n_corner, n_corner) - 1
         return pltpu.make_async_remote_copy(
-            src_ref=term.at[other // per_block],
-            dst_ref=landed.at[off - 1],
-            send_sem=term_send.at[off - 1],
-            recv_sem=term_recv.at[off - 1],
+            src_ref=term.at[block],
+            dst_ref=landed.at[slot],
+            send_sem=term_send.at[sent_as],
+            recv_sem=term_recv.at[slot],
             device_id={"corner": other},
             device_id_type=MESH,
         )
 
+    sends = []
+    half = blocks // 2
+    ahead = [half, half - 1, half + 1, half + 2] + [at for at in range(half - 2, 0, -1)]
+    ahead += [at for at in range(half + 3, blocks)] + [0]
+    for group in (ahead[:half], ahead[half:]):
+        places = [lax.rem(my_block + at, blocks) for at in group]
+        hi = jnp.concatenate([back_hi[place] for place in places], axis=0)
+        lo = jnp.concatenate([back_lo[place] for place in places], axis=0)
+        wide = dot(hi, back_col[...])
+        value = wide[:, :LANES] + wide[:, LANES:] + dot(lo, back_col[:, pl.ds(0, LANES)])
+        for at, place in enumerate(places):
+            term[place] = value[at * rows:(at + 1) * rows]
+        for at, place in zip(group, places):
+            for step in range(per_block):
+                if at == 0 and step == 0:
+                    continue
+                other = place * per_block + lax.rem(me_c + step, per_block)
+                copy = term_copy(place, other, len(sends))
+                copy.start()
+                sends.append(copy)
+    summed = term[my_block]
     for off in range(1, n_corner):
-        term_copy(off).start()
-    summed = term[me_c // per_block]
-    for off in range(1, n_corner):
-        term_copy(off).wait_recv()
+        term_copy(my_block, lax.rem(me_c + off, n_corner), off - 1).wait_recv()
         summed = summed + landed[off - 1]
     if per_block == 1:
         out_ref[...] = summed
@@ -521,8 +531,8 @@
             kept = kept + jnp.where(place == at, 1.0, 0.0) * summed[:, at * width:(at + 1) * width]
         out_ref[...] = kept
 
-    for off in range(1, n_corner):
-        term_copy(off).wait_send()
+    for copy in sends:
+        copy.wait_send()
     for off in range(1, n_space):
         share_copy(off).wait_send()
 
@@ -548,26 +558,32 @@
     reach = rows + 2 * HALO
     blocks = columns // LANES
     padded_rows = span + 2 * PAD
-    in_smem = pl.BlockSpec(memory_space=pltpu.SMEM)
+    in_hbm = pl.BlockSpec(memory_space=pltpu.HBM)
     in_vmem = pl.BlockSpec(memory_space=pltpu.VMEM)
     scratch = [
+        pltpu.SMEM(corner_set.shape, jnp.int32),
+        pltpu.SMEM(corner_dose.shape, f32),
+        pltpu.SMEM(kernel_weights.shape, f32),
+        pltpu.SMEM(force.shape, f32),
+        pltpu.VMEM(design.shape, f32),
+        pltpu.VMEM(kernel_taps.shape, f32),
+        pltpu.VMEM(design.shape, jnp.int32),
+        pltpu.VMEM(design.shape, jnp.int32),
         pltpu.VMEM((4 * kernels, LANES), f32),
         pltpu.VMEM((4 * kernels, LANES), f32),
         pltpu.VMEM((4 * kernels, LANES), f32),
-        pltpu.VMEM((kernels, 2 * LANES, 2 * LANES), bf16),
-        pltpu.VMEM((kernels, 2 * LANES, 2 * LANES), bf16),
-        pltpu.VMEM((kernels, 4 * LANES, 2 * LANES), bf16),
-        pltpu.VMEM((kernels, 2 * span, 2 * LANES), bf16),
-        pltpu.VMEM((kernels, 2 * span, 2 * LANES), bf16),
-        pltpu.VMEM((kernels, 2 * rows, 2 * LANES), bf16),
-        pltpu.VMEM((kernels, 2 * rows, 2 * LANES), bf16),
+        pltpu.VMEM((kernels, 6 * LANES, 2 * LANES), bf16),
+        pltpu.VMEM((kernels * 4 * LANES, 2 * LANES), bf16),
+        pltpu.VMEM((kernels, 4 * span, 2 * LANES), bf16),
+        pltpu.VMEM((kernels, 4 * rows, 2 * LANES), bf16),
         pltpu.VMEM((2 * HALO, columns), f32),
         pltpu.VMEM((2, 2 * MASK_HALO, columns), jnp.int32),
-        pltpu.VMEM((blocks * rows, 2 * LANES), bf16),
-        pltpu.VMEM((blocks * rows, 2 * LANES), bf16),
+        pltpu.VMEM((blocks * rows, 6 * LANES), bf16),
         pltpu.VMEM((kernels, 2 * reach, columns), bf16),
         pltpu.VMEM((kernels, 2 * reach, columns), bf16),
         pltpu.VMEM((kernels, 2 * span, columns), f32),
+        pltpu.VMEM((blocks, rows, kernels * 4 * LANES), bf16),
+        pltpu.VMEM((blocks, rows, kernels * 4 * LANES), bf16),
         pltpu.VMEM((padded_rows, columns), f32),
         pltpu.VMEM((span, columns), f32),
         pltpu.VMEM((padded_rows, columns), f32),
@@ -577,11 +593,11 @@
         pltpu.VMEM((padded_rows, columns), f32),
         pltpu.VMEM((span, columns), f32),
         pltpu.VMEM((span, columns), f32),
-        pltpu.VMEM((blocks * rows, LANES), f32),
         pltpu.VMEM((blocks, rows, LANES), f32),
         pltpu.VMEM((8, LANES), f32),
         pltpu.VMEM((n_space - 1, 8, LANES), f32),
         pltpu.VMEM((n_corner - 1, rows, LANES), f32),
+        pltpu.SemaphoreType.DMA((8,)),
         pltpu.SemaphoreType.DMA((2, 3)),
         pltpu.SemaphoreType.DMA((2, 3)),
         pltpu.SemaphoreType.DMA((n_space - 1,)),
@@ -592,11 +608,11 @@
     return pl.pallas_call(
         functools.partial(kernel, n_space, n_corner, kernels, radius),
         out_shape=jax.ShapeDtypeStruct((rows, columns // n_corner), f32),
-        in_specs=[in_smem] * 4 + [in_vmem] * 4,
+        in_specs=[in_hbm] * 8,
         out_specs=in_vmem,
         scratch_shapes=scratch,
         compiler_params=pltpu.CompilerParams(
-            collective_id=0, has_side_effects=True, vmem_limit_bytes=48 * 1024 * 1024
+            collective_id=0, has_side_effects=True, vmem_limit_bytes=56 * 1024 * 1024
         ),
     )(
         corner_set, corner_dose, kernel_weights, force,

time: 42.9 us -> 35.6 us (0.83)
  Pallas kernels: 37.1 us -> 32.8 us
  local copies, waits for them, and re-layouts: 4.23 us -> 1.35 us
    pallas_call x1, Pallas kernels: 37.1 us -> 32.8 us  [on_device(): pl.pallas_call(functools.partial(kernel, n_space, n_corner, kernels, radi...]
    unnamed x13 -> x1, local copies, waits for them, and re-layouts: 4.23 us -> 1.35 us
where the time goes in v2:
time: 35.6 us; the launch traced here: 35.4 us
  Pallas kernels  32.8 us (92%)
  local copies, waits for them, and re-layouts  1.35 us (4%)
  between operations  1.3 us (4%)
    pallas_call x1, Pallas kernels, on_device(): pl.pallas_call(functools.partial(kernel, n_space, n_corner, kernels, radi...  32.8 us
    unnamed x1, local copies, waits for them, and re-layouts  1.35 us

profile of v2, /device:TPU:0, one launch (start us, length us, event | category | flops | bytes accessed | tf_op | source)
XLA Modules:
  0.0 35.4 jit_solution(14692736380683063089)
XLA Ops:
  1.3 32.8 %shard_map.82 = f32[48,128]{1,0:T(8,128)} custom-call(s32[1]{0:T(128)S(6)} %copy.10.set_any, f32[1]{0:T(128)S(6)} %copy.11.dose_any, f32[4,8]{1,0:T(4,128)} %weight_any.1, f32[2]{0:T(128)} %force_any.1, f32[48,1024]{1,0:T(8,128)} %design_any.1, f32[4,4,8,17]{3,2,1,0:T(8,128)} %taps_any.1, s32[48,1024]{1,0:T(8,128)} %support_any.1, s32[48,1024]{1,0:T(8,128)} %load_any.1), custom_call_target="tpu_custom_call" | custom-call | tf_op jit(solution)/shard_map/pallas_call | solution.py:608
  34.1 1.3 %copy.12 = f32[48,128]{1,0:T(8,128)} copy(f32[48,128]{1,0:T(8,128)} %shard_map.82) | data formatting | bytes 49152

commit v3 on v2

--- a/solution.py
+++ b/solution.py
@@ -11,6 +11,7 @@
 MESH = pl.DeviceIdType.MESH
 LANES = 128
 HALO = 24
+TAIL = 18
 MASK_HALO = 16
 EDGE = 12
 PAD = 8
@@ -54,8 +55,8 @@
     out_ref,
     set_ref, dose_ref, weight_ref, force_ref, design_ref, taps_ref, support_ref, load_ref,
     tap_rows, base_plain, base_flip,
-    col_all, back_col, row_both, back_row_both,
-    halo, mask_halo, left_all, mid_hi, mid_lo, fields, back_hi, back_lo,
+    col_all, back_col, row_all, back_row_both,
+    halo, mask_halo, wide_design, stacked, stacked16, left_all, mid, fields, back_hi, back_lo, bright,
     stiff, ground, face_dn, face_rt, loads, image0, image1, factor, gain,
     term, share, shares, landed,
     local_sem, halo_send, halo_recv, share_send, share_recv, term_send, term_recv,
@@ -152,7 +153,7 @@
     near = jnp.abs(from_lane - to_lane) <= radius
     lane_row = lax.broadcasted_iota(jnp.int32, (span, LANES), 1)
     lane_out = lax.broadcasted_iota(jnp.int32, (rows, LANES), 1)
-    reach = rows + 2 * HALO
+    reach = rows + 2 * TAIL
 
     def build(at, carry):
         def plain(part):
@@ -184,17 +185,20 @@
 
         def forward_rows(part):
             band = circulant(flip(part), span, LANES - EDGE)
-            band = jnp.where(lane_row < rows + HALO, band, pltpu.roll(band, reach, 1))
-            return jnp.where(lane_row < reach, band, 0.0)
-
-        row_re = forward_rows(0)
-        row_im = forward_rows(1)
-        matrix = jnp.concatenate(
-            [joined(row_re, -row_im, lane_row, reach), joined(row_im, row_re, lane_row, reach)], axis=0
-        )
-        hi, lo = halves(matrix)
-        row_both[at, pl.ds(0, 2 * span), :] = hi
-        row_both[at, pl.ds(2 * span, 2 * span), :] = lo
+            band = jnp.where(lane_row < rows + TAIL, band, pltpu.roll(band, reach, 1))
+            band = jnp.where(lane_row < reach, band, 0.0)
+            hi = band.astype(bf16).astype(f32)
+            second = pltpu.roll(hi, reach, 1)
+            third = pltpu.roll(band - hi, 2 * reach - LANES, 1)
+            left = jnp.where(lane_row < reach, hi, second)
+            right = jnp.where(
+                lane_row < 2 * reach - LANES, second, jnp.where(lane_row < 3 * reach - LANES, third, 0.0)
+            )
+            return jnp.concatenate([left, right], axis=1)
+
+        row_all[pl.ds(pl.multiple_of(at * (2 * span), 16), 2 * span), :] = jnp.concatenate(
+            [forward_rows(0), forward_rows(1)], axis=0
+        ).astype(bf16)
         scale = 2.0 * weight_ref[chosen, at]
         row_re = circulant(plain(0), rows, EDGE) * scale
         row_im = circulant(plain(1), rows, EDGE) * scale
@@ -208,25 +212,8 @@
 
     lax.fori_loop(0, kernels, build, 0)
 
-    def columns_of(cells, begin):
-        parts = [cells[:, at * LANES:(at + 1) * LANES] for at in range(blocks)]
-        for at in range(blocks):
-            whole = jnp.concatenate([parts[at], side_lanes(parts, at)], axis=1)
-            hi, lo = halves(whole)
-            left_all[pl.ds(at * rows, rows), :] = jnp.concatenate([hi, hi, lo], axis=1)
-
-        for at in range(kernels):
-            value = dot(left_all[...], col_all[at])
-            hi, lo = halves(value)
-            for block in range(blocks):
-                for part in range(2):
-                    here = (slice(block * rows, (block + 1) * rows), slice(part * LANES, (part + 1) * LANES))
-                    there = (at, pl.ds(part * reach + begin, rows), pl.ds(block * LANES, LANES))
-                    mid_hi[there] = hi[here]
-                    mid_lo[there] = lo[here]
-
     local[5].wait()
-    columns_of(design_ref[...], 0)
+    wide_design[pl.ds(0, rows), :] = design_ref[...]
 
     @pl.when(has_after)
     def _():
@@ -248,12 +235,38 @@
         halo[pl.ds(HALO, HALO), :] = jnp.zeros((HALO, columns), f32)
         mask_halo[:, pl.ds(MASK_HALO, MASK_HALO), :] = jnp.zeros((2, MASK_HALO, columns), jnp.int32)
 
-    columns_of(halo[...], rows)
+    wide_design[pl.ds(rows, TAIL), :] = halo[pl.ds(0, TAIL), :]
+    wide_design[pl.ds(rows + TAIL, TAIL), :] = halo[pl.ds(2 * HALO - TAIL, TAIL), :]
+    cells = wide_design[pl.ds(0, reach), :]
+    high = cells.astype(bf16).astype(f32)
+    stacked[pl.ds(0, reach), :] = high
+    stacked[pl.ds(reach, reach), :] = cells - high
+    stacked[pl.ds(2 * reach, reach), :] = high
+    stacked[pl.ds(3 * reach, 2 * LANES - 3 * reach), :] = jnp.zeros((2 * LANES - 3 * reach, columns), f32)
+    stacked16[...] = stacked[...].astype(bf16)
+    for part in range(0, columns, 2 * LANES):
+        lanes = pl.ds(part, 2 * LANES)
+        mid[:, lanes] = dot(row_all[...], stacked16[:, lanes])
 
     for at in range(kernels):
-        both = row_both[at][:, :2 * reach]
-        of_high = dot(both, mid_hi[at])
-        fields[at] = of_high[:2 * span] + of_high[2 * span:] + dot(both[:2 * span], mid_lo[at])
+        left = left_all.at[at % 2]
+        value = mid[pl.ds(at * 2 * span, 2 * span), :]
+        parts = [value[:, block * LANES:(block + 1) * LANES] for block in range(blocks)]
+        for block in range(blocks):
+            hi, lo = halves(jnp.concatenate([parts[block], side_lanes(parts, block)], axis=1))
+            left[pl.ds(block * 2 * span, 2 * span), :] = jnp.concatenate([hi, hi, lo], axis=1)
+        value = dot(left[...], col_all[at])
+        weight = weight_ref[chosen, at]
+        for block in range(blocks):
+            of_re = value[block * 2 * span:block * 2 * span + span]
+            of_im = value[block * 2 * span + span:(block + 1) * 2 * span]
+            re = of_re[:, :LANES] - of_im[:, LANES:]
+            im = of_re[:, LANES:] + of_im[:, :LANES]
+            lanes = pl.ds(block * LANES, LANES)
+            fields[at, pl.ds(0, span), lanes] = re
+            fields[at, pl.ds(span, span), lanes] = im
+            light = weight * (re * re + im * im)
+            bright[:, lanes] = light if at == 0 else bright[:, lanes] + light
 
     for copy in local[6:]:
         copy.wait()
@@ -273,7 +286,6 @@
     grid_rows = n_space * rows
     low_end = math.tanh(beta_sharp * eta_level)
     spread = low_end + math.tanh(beta_sharp * (1.0 - eta_level))
-    weights = [weight_ref[chosen, at] for at in range(kernels)]
     level = dose / clear
     gain_scale = level * (3.0 * (1.0 - stiff_floor) * beta_sharp / spread)
 
@@ -290,13 +302,8 @@
 
     def project(strip, carry):
         begin = strip_of(strip)
-        bright = jnp.zeros((8, columns), f32)
-        for at in range(kernels):
-            re = fields[at, pl.ds(begin, 8), :]
-            im = fields[at, pl.ds(span + begin, 8), :]
-            bright = bright + weights[at] * (re * re + im * im)
-        bright = bright * level
-        bent = jnp.tanh(beta_sharp * (bright - eta_level))
+        light = bright[pl.ds(begin, 8), :] * level
+        bent = jnp.tanh(beta_sharp * (light - eta_level))
         density = (low_end + bent) * (1.0 / spread)
         square = density * density
         grid_row = row_in + (first_row + begin)
@@ -555,7 +562,6 @@
     kernels = kernel_taps.shape[2]
     radius = kernel_taps.shape[3] // 2
     span = rows + 2 * EDGE
-    reach = rows + 2 * HALO
     blocks = columns // LANES
     padded_rows = span + 2 * PAD
     in_hbm = pl.BlockSpec(memory_space=pltpu.HBM)
@@ -574,16 +580,19 @@
         pltpu.VMEM((4 * kernels, LANES), f32),
         pltpu.VMEM((kernels, 6 * LANES, 2 * LANES), bf16),
         pltpu.VMEM((kernels * 4 * LANES, 2 * LANES), bf16),
-        pltpu.VMEM((kernels, 4 * span, 2 * LANES), bf16),
+        pltpu.VMEM((kernels * 2 * span, 2 * LANES), bf16),
         pltpu.VMEM((kernels, 4 * rows, 2 * LANES), bf16),
         pltpu.VMEM((2 * HALO, columns), f32),
         pltpu.VMEM((2, 2 * MASK_HALO, columns), jnp.int32),
-        pltpu.VMEM((blocks * rows, 6 * LANES), bf16),
-        pltpu.VMEM((kernels, 2 * reach, columns), bf16),
-        pltpu.VMEM((kernels, 2 * reach, columns), bf16),
+        pltpu.VMEM((rows + 2 * HALO, columns), f32),
+        pltpu.VMEM((2 * LANES, columns), f32),
+        pltpu.VMEM((2 * LANES, columns), bf16),
+        pltpu.VMEM((2, blocks * 2 * span, 6 * LANES), bf16),
+        pltpu.VMEM((kernels * 2 * span, columns), f32),
         pltpu.VMEM((kernels, 2 * span, columns), f32),
         pltpu.VMEM((blocks, rows, kernels * 4 * LANES), bf16),
         pltpu.VMEM((blocks, rows, kernels * 4 * LANES), bf16),
+        pltpu.VMEM((span, columns), f32),
         pltpu.VMEM((padded_rows, columns), f32),
         pltpu.VMEM((span, columns), f32),
         pltpu.VMEM((padded_rows, columns), f32),

time: 35.6 us -> 36.6 us (1.028)
  Pallas kernels: 32.8 us -> 33.7 us
    pallas_call x1, Pallas kernels: 32.8 us -> 33.7 us  [on_device(): pl.pallas_call(functools.partial(kernel, n_space, n_corner, kernels, radi...]
where the time goes in v3:
time: 36.6 us; the launch traced here: 36.4 us
  Pallas kernels  33.7 us (92%)
  local copies, waits for them, and re-layouts  1.35 us (4%)
  between operations  1.3 us (4%)
    pallas_call x1, Pallas kernels, on_device(): pl.pallas_call(functools.partial(kernel, n_space, n_corner, kernels, radi...  33.7 us
    unnamed x1, local copies, waits for them, and re-layouts  1.35 us

profile of v3, /device:TPU:0, one launch (start us, length us, event | category | flops | bytes accessed | tf_op | source)
XLA Modules:
  0.0 36.4 jit_solution(3021759144041587692)
XLA Ops:
  1.3 33.7 %shard_map.82 = f32[48,128]{1,0:T(8,128)} custom-call(s32[1]{0:T(128)S(6)} %copy.10.set_any, f32[1]{0:T(128)S(6)} %copy.11.dose_any, f32[4,8]{1,0:T(4,128)} %weight_any.1, f32[2]{0:T(128)} %force_any.1, f32[48,1024]{1,0:T(8,128)} %design_any.1, f32[4,4,8,17]{3,2,1,0:T(8,128)} %taps_any.1, s32[48,1024]{1,0:T(8,128)} %support_any.1, s32[48,1024]{1,0:T(8,128)} %load_any.1), custom_call_target="tpu_custom_call" | custom-call | tf_op jit(solution)/shard_map/pallas_call | solution.py:617
  35.0 1.3 %copy.12 = f32[48,128]{1,0:T(8,128)} copy(f32[48,128]{1,0:T(8,128)} %shard_map.82) | data formatting | bytes 49152

commit v4 on v2

--- a/solution.py
+++ b/solution.py
@@ -55,7 +55,7 @@
     set_ref, dose_ref, weight_ref, force_ref, design_ref, taps_ref, support_ref, load_ref,
     tap_rows, base_plain, base_flip,
     col_all, back_col, row_both, back_row_both,
-    halo, mask_halo, left_all, mid_hi, mid_lo, fields, back_hi, back_lo,
+    halo, mask_halo, left_all, mid_hi, mid_lo, fields, back_hi, back_lo, sides_held, bright,
     stiff, ground, face_dn, face_rt, loads, image0, image1, factor, gain,
     term, share, shares, landed,
     local_sem, halo_send, halo_recv, share_send, share_recv, term_send, term_recv,
@@ -162,19 +162,36 @@
             return base_flip[pl.ds(part * kernels + at, 1), :]
 
         for part in range(2):
+            there = pl.ds(part * LANES, LANES)
             band = circulant(plain(2 + part), LANES, 0)
-            hi, lo = halves(band)
-            zero = jnp.zeros_like(hi)
-            there = pl.ds(part * LANES, LANES)
-            for place, value in ((0, hi), (1, lo), (2, hi)):
-                col_all[at, pl.ds(2 * place * LANES, LANES), there] = jnp.where(near, value, zero)
-                col_all[at, pl.ds((2 * place + 1) * LANES, LANES), there] = jnp.where(near, zero, value)
+            hi = band.astype(bf16).astype(f32)
+            lo = band - hi
+            far_hi = jnp.where(near, 0.0, hi)
+            far_lo = jnp.where(near, 0.0, lo)
+            near_hi = jnp.where(near, hi, 0.0).astype(bf16)
+            col_all[at, pl.ds(0, LANES), there] = near_hi
+            col_all[at, pl.ds(LANES, LANES), there] = near_hi
+            col_all[at, pl.ds(2 * LANES, LANES), there] = jnp.where(near, lo, 0.0).astype(bf16)
+            col_all[at, pl.ds(3 * LANES, LANES), there] = (
+                far_hi + pltpu.roll(far_hi, 2 * radius, 0) + pltpu.roll(far_lo, 4 * radius, 0)
+            ).astype(bf16)
             band = circulant(flip(2 + part), LANES, 0)
-            hi, lo = halves(band)
-            for value, lanes in ((hi, 0), (lo, LANES)):
-                place = pl.multiple_of(at * (4 * LANES), LANES) + 2 * part * LANES
-                back_col[pl.ds(place, LANES), pl.ds(lanes, LANES)] = jnp.where(near, value, zero)
-                back_col[pl.ds(place + LANES, LANES), pl.ds(lanes, LANES)] = jnp.where(near, zero, value)
+            hi = band.astype(bf16).astype(f32)
+            lo = band - hi
+            field = 2 * at + part
+            begin = pl.multiple_of(field * LANES, LANES)
+            back_col[pl.ds(begin, LANES), pl.ds(0, LANES)] = jnp.where(near, hi, 0.0).astype(bf16)
+            back_col[pl.ds(begin, LANES), pl.ds(LANES, LANES)] = jnp.where(near, lo, 0.0).astype(bf16)
+            far = jnp.concatenate([jnp.where(near, 0.0, hi), jnp.where(near, 0.0, lo)], axis=1)
+            far = jnp.concatenate([far[LANES - radius:], far[:radius]], axis=0)
+            begin = pl.multiple_of(2 * kernels * LANES + field * 2 * radius, 2 * radius)
+            back_col[pl.ds(begin, 2 * radius), :] = far.astype(bf16)
+            back_col[pl.ds(begin + 4 * kernels * radius, 2 * radius), pl.ds(0, LANES)] = (
+                far[:, :LANES].astype(bf16)
+            )
+            back_col[pl.ds(begin + 4 * kernels * radius, 2 * radius), pl.ds(LANES, LANES)] = (
+                jnp.zeros((2 * radius, LANES), bf16)
+            )
 
         def joined(first, second, lane, width):
             turned = pltpu.roll(second, width, 1)
@@ -211,9 +228,19 @@
     def columns_of(cells, begin):
         parts = [cells[:, at * LANES:(at + 1) * LANES] for at in range(blocks)]
         for at in range(blocks):
-            whole = jnp.concatenate([parts[at], side_lanes(parts, at)], axis=1)
-            hi, lo = halves(whole)
-            left_all[pl.ds(at * rows, rows), :] = jnp.concatenate([hi, hi, lo], axis=1)
+            hi, lo = halves(parts[at])
+            side = side_lanes(parts, at)
+            side_hi = side.astype(bf16).astype(f32)
+            packed = jnp.where(
+                (lane_out < radius) | (lane_out >= LANES - radius),
+                side_hi,
+                jnp.where(
+                    lane_out < 3 * radius,
+                    pltpu.roll(side - side_hi, 2 * radius, 1),
+                    jnp.where(lane_out < 5 * radius, pltpu.roll(side_hi, 4 * radius, 1), 0.0),
+                ),
+            )
+            left_all[pl.ds(at * rows, rows), :] = jnp.concatenate([hi, lo, hi, packed.astype(bf16)], axis=1)
 
         for at in range(kernels):
             value = dot(left_all[...], col_all[at])
@@ -253,7 +280,10 @@
     for at in range(kernels):
         both = row_both[at][:, :2 * reach]
         of_high = dot(both, mid_hi[at])
-        fields[at] = of_high[:2 * span] + of_high[2 * span:] + dot(both[:2 * span], mid_lo[at])
+        value = of_high[:2 * span] + of_high[2 * span:] + dot(both[:2 * span], mid_lo[at])
+        fields[at] = value
+        light = weight_ref[chosen, at] * (value[:span] * value[:span] + value[span:] * value[span:])
+        bright[...] = light if at == 0 else bright[...] + light
 
     for copy in local[6:]:
         copy.wait()
@@ -273,7 +303,6 @@
     grid_rows = n_space * rows
     low_end = math.tanh(beta_sharp * eta_level)
     spread = low_end + math.tanh(beta_sharp * (1.0 - eta_level))
-    weights = [weight_ref[chosen, at] for at in range(kernels)]
     level = dose / clear
     gain_scale = level * (3.0 * (1.0 - stiff_floor) * beta_sharp / spread)
 
@@ -290,13 +319,8 @@
 
     def project(strip, carry):
         begin = strip_of(strip)
-        bright = jnp.zeros((8, columns), f32)
-        for at in range(kernels):
-            re = fields[at, pl.ds(begin, 8), :]
-            im = fields[at, pl.ds(span + begin, 8), :]
-            bright = bright + weights[at] * (re * re + im * im)
-        bright = bright * level
-        bent = jnp.tanh(beta_sharp * (bright - eta_level))
+        light = bright[pl.ds(begin, 8), :] * level
+        bent = jnp.tanh(beta_sharp * (light - eta_level))
         density = (low_end + bent) * (1.0 / spread)
         square = density * density
         grid_row = row_in + (first_row + begin)
@@ -478,10 +502,26 @@
             piece = turned[part * rows:(part + 1) * rows]
             parts = [piece[:, block * LANES:(block + 1) * LANES] for block in range(blocks)]
             for block in range(blocks):
-                hi, lo = halves(jnp.concatenate([parts[block], side_lanes(parts, block)], axis=1))
-                lanes = pl.ds((2 * at + part) * 2 * LANES, 2 * LANES)
+                field = 2 * at + part
+                hi, lo = halves(parts[block])
+                lanes = pl.ds(field * LANES, LANES)
                 back_hi[block, :, lanes] = hi
                 back_lo[block, :, lanes] = lo
+                edge = side_lanes(parts, block)
+                edge_hi = edge.astype(bf16).astype(f32)
+                slots = LANES // (2 * radius)
+                place = field % slots
+                turn = radius + place * 2 * radius
+                keep = lane_out // (2 * radius) == place
+                for group, cells in ((field // slots, edge_hi), (2 * kernels // slots + field // slots, edge - edge_hi)):
+                    moved = pltpu.roll(cells, turn % LANES, 1)
+                    lanes = pl.ds(group * LANES, LANES)
+                    moved = jnp.where(keep, moved, 0.0 if place == 0 else sides_held[block, :, lanes])
+                    if place == slots - 1:
+                        lanes = pl.ds((2 * kernels + group) * LANES, LANES)
+                        back_hi[block, :, lanes] = moved.astype(bf16)
+                    else:
+                        sides_held[block, :, lanes] = moved
 
     width = columns // n_corner
     per_block = LANES // width
@@ -507,7 +547,7 @@
         hi = jnp.concatenate([back_hi[place] for place in places], axis=0)
         lo = jnp.concatenate([back_lo[place] for place in places], axis=0)
         wide = dot(hi, back_col[...])
-        value = wide[:, :LANES] + wide[:, LANES:] + dot(lo, back_col[:, pl.ds(0, LANES)])
+        value = wide[:, :LANES] + wide[:, LANES:] + dot(lo, back_col[pl.ds(0, 2 * kernels * LANES), pl.ds(0, LANES)])
         for at, place in enumerate(places):
             term[place] = value[at * rows:(at + 1) * rows]
         for at, place in zip(group, places):
@@ -572,18 +612,20 @@
         pltpu.VMEM((4 * kernels, LANES), f32),
         pltpu.VMEM((4 * kernels, LANES), f32),
         pltpu.VMEM((4 * kernels, LANES), f32),
-        pltpu.VMEM((kernels, 6 * LANES, 2 * LANES), bf16),
-        pltpu.VMEM((kernels * 4 * LANES, 2 * LANES), bf16),
+        pltpu.VMEM((kernels, 4 * LANES, 2 * LANES), bf16),
+        pltpu.VMEM((2 * kernels * (LANES + 4 * radius), 2 * LANES), bf16),
         pltpu.VMEM((kernels, 4 * span, 2 * LANES), bf16),
         pltpu.VMEM((kernels, 4 * rows, 2 * LANES), bf16),
         pltpu.VMEM((2 * HALO, columns), f32),
         pltpu.VMEM((2, 2 * MASK_HALO, columns), jnp.int32),
-        pltpu.VMEM((blocks * rows, 6 * LANES), bf16),
+        pltpu.VMEM((blocks * rows, 4 * LANES), bf16),
         pltpu.VMEM((kernels, 2 * reach, columns), bf16),
         pltpu.VMEM((kernels, 2 * reach, columns), bf16),
         pltpu.VMEM((kernels, 2 * span, columns), f32),
-        pltpu.VMEM((blocks, rows, kernels * 4 * LANES), bf16),
-        pltpu.VMEM((blocks, rows, kernels * 4 * LANES), bf16),
+        pltpu.VMEM((blocks, rows, 2 * kernels * (LANES + 4 * radius)), bf16),
+        pltpu.VMEM((blocks, rows, 2 * kernels * LANES), bf16),
+        pltpu.VMEM((blocks, rows, 8 * kernels * radius), f32),
+        pltpu.VMEM((span, columns), f32),
         pltpu.VMEM((padded_rows, columns), f32),
         pltpu.VMEM((span, columns), f32),
         pltpu.VMEM((padded_rows, columns), f32),

time: 35.6 us -> 34.9 us (0.980)
  Pallas kernels: 32.8 us -> 32.1 us
    pallas_call x1, Pallas kernels: 32.8 us -> 32.1 us  [on_device(): pl.pallas_call(functools.partial(kernel, n_space, n_corner, kernels, radi...]
where the time goes in v4:
time: 34.9 us; the launch traced here: 34.7 us
  Pallas kernels  32.1 us (92%)
  local copies, waits for them, and re-layouts  1.35 us (4%)
  between operations  1.3 us (4%)
    pallas_call x1, Pallas kernels, on_device(): pl.pallas_call(functools.partial(kernel, n_space, n_corner, kernels, radi...  32.1 us
    unnamed x1, local copies, waits for them, and re-layouts  1.35 us

profile of v4, /device:TPU:0, one launch (start us, length us, event | category | flops | bytes accessed | tf_op | source)
XLA Modules:
  0.0 34.7 jit_solution(5708579682160689022)
XLA Ops:
  1.3 32.1 %shard_map.82 = f32[48,128]{1,0:T(8,128)} custom-call(s32[1]{0:T(128)S(6)} %copy.10.set_any, f32[1]{0:T(128)S(6)} %copy.11.dose_any, f32[4,8]{1,0:T(4,128)} %weight_any.1, f32[2]{0:T(128)} %force_any.1, f32[48,1024]{1,0:T(8,128)} %design_any.1, f32[4,4,8,17]{3,2,1,0:T(8,128)} %taps_any.1, s32[48,1024]{1,0:T(8,128)} %support_any.1, s32[48,1024]{1,0:T(8,128)} %load_any.1), custom_call_target="tpu_custom_call" | custom-call | tf_op jit(solution)/shard_map/pallas_call | solution.py:650
  33.4 1.3 %copy.12 = f32[48,128]{1,0:T(8,128)} copy(f32[48,128]{1,0:T(8,128)} %shard_map.82) | data formatting | bytes 49152

commit v5 on v4

--- a/solution.py
+++ b/solution.py
@@ -289,7 +289,7 @@
         copy.wait()
 
     zero_pad = jnp.zeros((PAD, columns), f32)
-    for array in (stiff, face_dn, loads, image0, image1):
+    for array in (stiff, loads, image0, image1):
         array[pl.ds(0, PAD), :] = zero_pad
         array[pl.ds(PAD + span, PAD), :] = zero_pad
     for which_one, own, target, base in ((0, load_ref, loads, PAD), (1, support_ref, ground, 0)):
@@ -308,14 +308,6 @@
 
     def strip_of(strip):
         return pl.multiple_of(strip * 8, 8)
-
-    def row_above(array, begin, here):
-        before = array[pl.ds(begin + PAD - 8, 8), :]
-        return jnp.where(row_in == 0, pltpu.roll(before, 1, 0), pltpu.roll(here, 1, 0))
-
-    def row_below(array, begin, here):
-        after = array[pl.ds(begin + PAD + 8, 8), :]
-        return jnp.where(row_in == 7, pltpu.roll(after, 7, 0), pltpu.roll(here, 7, 0))
 
     def project(strip, carry):
         begin = strip_of(strip)
@@ -335,59 +327,60 @@
 
     lax.fori_loop(0, strips, project, 0)
 
-    def faces(strip, carry):
-        begin = strip_of(strip)
-        here = stiff[pl.ds(begin + PAD, 8), :]
-        below = row_below(stiff, begin, here)
-        face_dn[pl.ds(begin + PAD, 8), :] = 2.0 * here * below / jnp.maximum(here + below, 1e-20)
-        right = pltpu.roll(here, columns - 1, 1)
-        face = 2.0 * here * right / jnp.maximum(here + right, 1e-20)
-        face_rt[pl.ds(begin, 8), :] = jnp.where(lane_in < columns - 1, face, 0.0)
-        return carry
-
-    lax.fori_loop(0, strips, faces, 0)
-
     force0 = force_ref[0]
     force1 = force_ref[1]
 
-    def around(strip):
+    def two(array, strip):
         begin = strip_of(strip)
-        right = face_rt[pl.ds(begin, 8), :]
-        down = face_dn[pl.ds(begin + PAD, 8), :]
-        return row_above(face_dn, begin, down), down, pltpu.roll(right, 1, 1), right
-
-    def three(array, strip):
-        begin = strip_of(strip)
-        here = array[pl.ds(begin + PAD, 8), :]
-        return row_above(array, begin, here), here, row_below(array, begin, here)
+        return array[pl.ds(begin + PAD, 8), :], array[pl.ds(begin + PAD + 8, 8), :]
+
+    def row_below(here, after):
+        return jnp.where(row_in == 7, pltpu.roll(after, 7, 0), pltpu.roll(here, 7, 0))
+
+    def row_above(here, before):
+        return jnp.where(row_in == 0, pltpu.roll(before, 1, 0), pltpu.roll(here, 1, 0))
+
+    def on_right(here):
+        return pltpu.roll(here, columns - 1, 1)
+
+    def on_left(here):
+        return pltpu.roll(here, 1, 1)
 
     def own_rows(strip):
         row = row_in + strip_of(strip)
         return (row >= EDGE) & (row < EDGE + rows)
 
-    def flows(above, here, below, sides):
-        face_up, face_down, face_left, face_right = sides
-        along_rows = face_up * (here - above) + face_down * (here - below)
-        along_columns = face_left * (here - pltpu.roll(here, 1, 1)) + face_right * (
-            here - pltpu.roll(here, columns - 1, 1)
-        )
-        return along_rows, along_columns
+    def folded(cells):
+        return sum(cells[:, block * LANES:(block + 1) * LANES] for block in range(blocks))
+
+    blank = jnp.zeros((8, columns), f32)
+    narrow = jnp.zeros((8, LANES), f32)
 
     def first_image(strip, carry):
-        norm, energy = carry
+        flux_before, norm, energy = carry
         begin = strip_of(strip)
-        above, here, below = three(loads, strip)
-        along_rows, along_columns = flows(above, here, below, around(strip))
+        hard, hard_after = two(stiff, strip)
+        hard_below = row_below(hard, hard_after)
+        hard_right = on_right(hard)
+        face_down = 2.0 * hard * hard_below / jnp.maximum(hard + hard_below, 1e-20)
+        face_right = 2.0 * hard * hard_right / jnp.maximum(hard + hard_right, 1e-20)
+        face_right = jnp.where(lane_in < columns - 1, face_right, 0.0)
+        face_dn[pl.ds(begin, 8), :] = face_down
+        face_rt[pl.ds(begin, 8), :] = face_right
+        here, after = two(loads, strip)
+        flux = face_down * (here - row_below(here, after))
+        along_rows = flux - row_above(flux, flux_before)
+        across = face_right * (here - on_right(here))
+        along_columns = across - on_left(across)
         held = ground[pl.ds(begin, 8), :] * here
         one = force0 * (held + along_rows + shear * along_columns)
-        two = force1 * (held + shear * along_rows + along_columns)
+        other = force1 * (held + shear * along_rows + along_columns)
         image0[pl.ds(begin + PAD, 8), :] = one
-        image1[pl.ds(begin + PAD, 8), :] = two
+        image1[pl.ds(begin + PAD, 8), :] = other
         own = jnp.where(own_rows(strip), here, 0.0)
-        return norm + own * own, energy + own * (force0 * one + force1 * two)
-
-    blank = jnp.zeros((8, columns), f32)
-    norm, energy = lax.fori_loop(0, strips, first_image, (blank, blank))
+        return flux, norm + folded(own * own), energy + folded(own * (force0 * one + force1 * other))
+
+    flux, norm, energy = lax.fori_loop(0, strips, first_image, (blank, narrow, narrow))
 
     def whole_sum(cells):
         return jnp.sum(jnp.sum(cells, axis=0, keepdims=True), axis=1, keepdims=True)
@@ -397,28 +390,36 @@
     ratio = jnp.where(norm > 0.0, energy / jnp.where(norm > 0.0, norm, 1.0), 0.0)
 
     def second_image(strip, carry):
-        sums = list(carry)
-        sides = around(strip)
-        load3 = three(loads, strip)
-        held = ground[pl.ds(strip_of(strip), 8), :]
+        flux_before, sums = list(carry[:2]), list(carry[2:])
+        begin = strip_of(strip)
+        face_down = face_dn[pl.ds(begin, 8), :]
+        face_right = face_rt[pl.ds(begin, 8), :]
+        load, load_after = two(loads, strip)
+        held = ground[pl.ds(begin, 8), :]
         keep = own_rows(strip)
-        for array, push, of_rows, of_columns in (
+        for at, (array, push, of_rows, of_columns) in enumerate((
             (image0, force0, 1.0, shear), (image1, force1, shear, 1.0)
-        ):
-            image3 = three(array, strip)
+        )):
+            image, image_after = two(array, strip)
             lean = ratio * push
-            above, here, below = [image3[at] - lean * load3[at] for at in range(3)]
-            along_rows, along_columns = flows(above, here, below, sides)
+            here = image - lean * load
+            flux = face_down * (here - row_below(here, image_after - lean * load_after))
+            along_rows = flux - row_above(flux, flux_before[at])
+            flux_before[at] = flux
+            across = face_right * (here - on_right(here))
+            along_columns = across - on_left(across)
             applied = held * here + of_rows * along_rows + of_columns * along_columns
             applied = jnp.where(keep, applied, 0.0)
-            sums[0] = sums[0] + jnp.where(keep, here * here, 0.0)
-            sums[1] = sums[1] + here * applied
-            sums[2] = sums[2] + push * load3[1] * applied
-        return tuple(sums)
+            sums[0] = sums[0] + folded(jnp.where(keep, here * here, 0.0))
+            sums[1] = sums[1] + folded(here * applied)
+            sums[2] = sums[2] + push * folded(load * applied)
+        return tuple(flux_before + sums)
 
     first_strip = EDGE // 8
     last_strip = (EDGE + rows + 7) // 8
-    rest = lax.fori_loop(first_strip, last_strip, second_image, (blank, blank, blank))
+    rest = lax.fori_loop(
+        first_strip, last_strip, second_image, (blank, blank, narrow, narrow, narrow)
+    )[2:]
     values = [norm, ratio] + [whole_sum(cells) for cells in rest]
     lane8 = lax.broadcasted_iota(jnp.int32, (8, LANES), 1)
     packed = jnp.zeros((8, LANES), f32)
@@ -458,36 +459,34 @@
     of_load = inverse + step * (1.0 + renew)
     of_image = -step * inverse
 
-    def slopes(strip, carry):
+    def slopes(strip, bend_before):
         begin = strip_of(strip)
-        sides = around(strip)
-        squares = [side * side for side in sides]
-        load3 = three(loads, strip)
-        here_stiff = stiff[pl.ds(begin + PAD, 8), :]
+        face_down = face_dn[pl.ds(begin, 8), :]
+        face_right = face_rt[pl.ds(begin, 8), :]
+        load, load_after = two(loads, strip)
+        hard = stiff[pl.ds(begin + PAD, 8), :]
         held = jnp.zeros((8, columns), f32)
-        bent = jnp.zeros((8, columns), f32)
+        bend_down = jnp.zeros((8, columns), f32)
+        bend_right = jnp.zeros((8, columns), f32)
         for array, push, of_rows, of_columns in (
             (image0, force0, 1.0, shear), (image1, force1, shear, 1.0)
         ):
-            image3 = three(array, strip)
-            above, here, below = [
-                (of_load * push) * load3[at] + of_image * image3[at] for at in range(3)
-            ]
-            up = here - above
-            down = here - below
-            left = here - pltpu.roll(here, 1, 1)
-            right = here - pltpu.roll(here, columns - 1, 1)
+            image, image_after = two(array, strip)
+            lean = of_load * push
+            here = lean * load + of_image * image
+            down = here - row_below(here, lean * load_after + of_image * image_after)
+            right = here - on_right(here)
             held = held + here * here
-            bent = (
-                bent
-                + of_rows * (squares[0] * (up * up) + squares[1] * (down * down))
-                + of_columns * (squares[2] * (left * left) + squares[3] * (right * right))
-            )
-        bent = bent * 0.5 / jnp.maximum(here_stiff * here_stiff, 1e-6)
+            bend_down = bend_down + of_rows * (down * down)
+            bend_right = bend_right + of_columns * (right * right)
+        bend_down = face_down * face_down * bend_down
+        bend_right = face_right * face_right * bend_right
+        bent = bend_down + row_above(bend_down, bend_before) + bend_right + on_left(bend_right)
+        bent = bent * 0.5 / jnp.maximum(hard * hard, 1e-6)
         gain[pl.ds(begin, 8), :] = factor[pl.ds(begin, 8), :] * (kappa_ground * held + bent)
-        return carry
-
-    lax.fori_loop(0, strips, slopes, 0)
+        return bend_down
+
+    lax.fori_loop(0, strips, slopes, blank)
 
     for at in range(kernels):
         scale = gain[...]

time: 34.9 us -> 35.5 us (1.017)
  Pallas kernels: 32.1 us -> 32.6 us
    pallas_call x1, Pallas kernels: 32.1 us -> 32.6 us  [on_device(): pl.pallas_call(functools.partial(kernel, n_space, n_corner, kernels, radi...]
where the time goes in v5:
time: 35.5 us; the launch traced here: 35.3 us
  Pallas kernels  32.6 us (92%)
  local copies, waits for them, and re-layouts  1.35 us (4%)
  between operations  1.3 us (4%)
    pallas_call x1, Pallas kernels, on_device(): pl.pallas_call(functools.partial(kernel, n_space, n_corner, kernels, radi...  32.6 us
    unnamed x1, local copies, waits for them, and re-layouts  1.35 us

profile of v5, /device:TPU:0, one launch (start us, length us, event | category | flops | bytes accessed | tf_op | source)
XLA Modules:
  0.0 35.3 jit_solution(14858084936096875973)
XLA Ops:
  1.3 32.6 %shard_map.82 = f32[48,128]{1,0:T(8,128)} custom-call(s32[1]{0:T(128)S(6)} %copy.10.set_any, f32[1]{0:T(128)S(6)} %copy.11.dose_any, f32[4,8]{1,0:T(4,128)} %weight_any.1, f32[2]{0:T(128)} %force_any.1, f32[48,1024]{1,0:T(8,128)} %design_any.1, f32[4,4,8,17]{3,2,1,0:T(8,128)} %taps_any.1, s32[48,1024]{1,0:T(8,128)} %support_any.1, s32[48,1024]{1,0:T(8,128)} %load_any.1), custom_call_target="tpu_custom_call" | custom-call | tf_op jit(solution)/shard_map/pallas_call | solution.py:649
  33.9 1.3 %copy.12 = f32[48,128]{1,0:T(8,128)} copy(f32[48,128]{1,0:T(8,128)} %shard_map.82) | data formatting | bytes 49152

commit v6 on v5

--- a/solution.py
+++ b/solution.py
@@ -223,7 +223,7 @@
         back_row_both[at, pl.ds(2 * rows, 2 * rows), :] = lo
         return carry
 
-    lax.fori_loop(0, kernels, build, 0)
+    lax.fori_loop(0, kernels, build, 0, unroll=True)
 
     def columns_of(cells, begin):
         parts = [cells[:, at * LANES:(at + 1) * LANES] for at in range(blocks)]
@@ -325,7 +325,7 @@
         )
         return carry
 
-    lax.fori_loop(0, strips, project, 0)
+    lax.fori_loop(0, strips, project, 0, unroll=True)
 
     force0 = force_ref[0]
     force1 = force_ref[1]
@@ -380,7 +380,7 @@
         own = jnp.where(own_rows(strip), here, 0.0)
         return flux, norm + folded(own * own), energy + folded(own * (force0 * one + force1 * other))
 
-    flux, norm, energy = lax.fori_loop(0, strips, first_image, (blank, narrow, narrow))
+    flux, norm, energy = lax.fori_loop(0, strips, first_image, (blank, narrow, narrow), unroll=True)
 
     def whole_sum(cells):
         return jnp.sum(jnp.sum(cells, axis=0, keepdims=True), axis=1, keepdims=True)
@@ -418,7 +418,7 @@
     first_strip = EDGE // 8
     last_strip = (EDGE + rows + 7) // 8
     rest = lax.fori_loop(
-        first_strip, last_strip, second_image, (blank, blank, narrow, narrow, narrow)
+        first_strip, last_strip, second_image, (blank, blank, narrow, narrow, narrow), unroll=True
     )[2:]
     values = [norm, ratio] + [whole_sum(cells) for cells in rest]
     lane8 = lax.broadcasted_iota(jnp.int32, (8, LANES), 1)
@@ -486,7 +486,7 @@
         gain[pl.ds(begin, 8), :] = factor[pl.ds(begin, 8), :] * (kappa_ground * held + bent)
         return bend_down
 
-    lax.fori_loop(0, strips, slopes, blank)
+    lax.fori_loop(0, strips, slopes, blank, unroll=True)
 
     for at in range(kernels):
         scale = gain[...]

time: 35.5 us -> 32.2 us (0.907)
  Pallas kernels: 32.6 us -> 29.3 us
    pallas_call x1, Pallas kernels: 32.6 us -> 29.3 us  [on_device(): pl.pallas_call(functools.partial(kernel, n_space, n_corner, kernels, radi...]
where the time goes in v6:
time: 32.2 us; the launch traced here: 32 us
  Pallas kernels  29.3 us (91%)
  local copies, waits for them, and re-layouts  1.35 us (4%)
  between operations  1.3 us (4%)
    pallas_call x1, Pallas kernels, on_device(): pl.pallas_call(functools.partial(kernel, n_space, n_corner, kernels, radi...  29.3 us
    unnamed x1, local copies, waits for them, and re-layouts  1.35 us

profile of v6, /device:TPU:0, one launch (start us, length us, event | category | flops | bytes accessed | tf_op | source)
XLA Modules:
  0.0 32.0 jit_solution(2549936352326896910)
XLA Ops:
  1.3 29.3 %shard_map.82 = f32[48,128]{1,0:T(8,128)} custom-call(s32[1]{0:T(128)S(6)} %copy.10.set_any, f32[1]{0:T(128)S(6)} %copy.11.dose_any, f32[4,8]{1,0:T(4,128)} %weight_any.1, f32[2]{0:T(128)} %force_any.1, f32[48,1024]{1,0:T(8,128)} %design_any.1, f32[4,4,8,17]{3,2,1,0:T(8,128)} %taps_any.1, s32[48,1024]{1,0:T(8,128)} %support_any.1, s32[48,1024]{1,0:T(8,128)} %load_any.1), custom_call_target="tpu_custom_call" | custom-call | tf_op jit(solution)/shard_map/pallas_call | solution.py:649
  30.6 1.3 %copy.12 = f32[48,128]{1,0:T(8,128)} copy(f32[48,128]{1,0:T(8,128)} %shard_map.82) | data formatting | bytes 49152
